TPU v7x, 32 devices: a whole 2x2x4 slice. The times are simulated.
32 devices in a mesh: row: 4 (over y, x), head: 4 (over z), seq: 2 (over core).
Axes of the slice: x: 2, y: 2, z: 4, core: 2. Of those that a mesh axis runs over, the one named last changes fastest.
Arguments:
- tokens: bfloat16 [16, 512, 768], P(('row', 'seq'), 'head'), may hold values from -6 to 6
- lengths: int32 [16], P(('row', 'seq')), may hold values from 461 to 512, as said below
- cotangent: bfloat16 [16, 512, 768], P(('row', 'seq'), 'head'), may hold values from -6 to 6
- t_query: bfloat16 [768, 768], P(None, 'head'), may hold values from -0.21875 to 0.21875
- t_query_bias: float32 [768], P('head'), may hold values from -3 to 3
- t_key: bfloat16 [768, 768], P(None, 'head'), may hold values from -0.21875 to 0.21875
- t_value: bfloat16 [768, 768], P(None, 'head'), may hold values from -0.21875 to 0.21875
- t_value_bias: float32 [768], P('head'), may hold values from -3 to 3
- t_attn_out: bfloat16 [768, 768], P('head'), may hold values from -0.875 to 0.875
- t_attn_bias: float32 [768], replicated, may hold values from -3 to 3
- t_norm1_gain: float32 [768], replicated, may hold values from 0.1 to 1.9
- t_norm1_bias: float32 [768], replicated, may hold values from -2 to 2
- t_ffn_in: bfloat16 [768, 3072], P(None, ('head', 'seq')), may hold values from -0.21875 to 0.21875
- t_ffn_in_bias: bfloat16 [3072], P(('head', 'seq')), may hold values from -3 to 3
- t_ffn_out: bfloat16 [3072, 768], P(('head', 'seq')), may hold values from -0.109375 to 0.109375
- t_ffn_out_bias: float32 [768], replicated, may hold values from -3 to 3
- t_norm2_gain: float32 [768], replicated, may hold values from 0.1 to 1.9
- t_norm2_bias: float32 [768], replicated, may hold values from -2 to 2
- s_query: bfloat16 [768, 384], replicated, may hold values from -0.21875 to 0.21875
- s_query_bias: float32 [384], replicated, may hold values from -3 to 3
- s_key: bfloat16 [768, 384], replicated, may hold values from -0.21875 to 0.21875
- s_value: bfloat16 [768, 384], replicated, may hold values from -0.21875 to 0.21875
- s_value_bias: float32 [384], replicated, may hold values from -3 to 3
- s_attn_out: bfloat16 [384, 768], replicated, may hold values from -1.25 to 1.25
- s_attn_bias: float32 [768], replicated, may hold values from -3 to 3
- s_norm1_gain: float32 [768], replicated, may hold values from 0.1 to 1.9
- s_norm1_bias: float32 [768], replicated, may hold values from -2 to 2
- s_ffn_in: bfloat16 [768, 1536], P(None, ('head', 'seq')), may hold values from -0.21875 to 0.21875
- s_ffn_in_bias: bfloat16 [1536], P(('head', 'seq')), may hold values from -3 to 3
- s_ffn_out: bfloat16 [1536, 768], P(('head', 'seq')), may hold values from -0.15625 to 0.15625
- s_ffn_out_bias: float32 [768], replicated, may hold values from -3 to 3
- s_norm2_gain: float32 [768], replicated, may hold values from 0.1 to 1.9
- s_norm2_bias: float32 [768], replicated, may hold values from -2 to 2
Outputs:
- output: float32 [16, 512, 768], P(('row', 'seq'), 'head')
- input_grad: float32 [16, 512, 768], P(('row', 'seq'), 'head')
- grad_t_query: float32 [768, 768], P(None, 'head')
- grad_t_query_bias: float32 [768], P('head')
- grad_t_key: float32 [768, 768], P(None, 'head')
- grad_t_value: float32 [768, 768], P(None, 'head')
- grad_t_value_bias: float32 [768], P('head')
- grad_t_attn_out: float32 [768, 768], P('head')
- grad_t_attn_bias: float32 [768], replicated
- grad_t_norm1_gain: float32 [768], replicated
- grad_t_norm1_bias: float32 [768], replicated
- grad_t_ffn_in: float32 [768, 3072], P(None, ('head', 'seq'))
- grad_t_ffn_in_bias: float32 [3072], P(('head', 'seq'))
- grad_t_ffn_out: float32 [3072, 768], P(('head', 'seq'))
- grad_t_ffn_out_bias: float32 [768], replicated
- grad_t_norm2_gain: float32 [768], replicated
- grad_t_norm2_bias: float32 [768], replicated
- grad_s_query: float32 [768, 384], replicated
- grad_s_query_bias: float32 [384], replicated
- grad_s_key: float32 [768, 384], replicated
- grad_s_value: float32 [768, 384], replicated
- grad_s_value_bias: float32 [384], replicated
- grad_s_attn_out: float32 [384, 768], replicated
- grad_s_attn_bias: float32 [768], replicated
- grad_s_norm1_gain: float32 [768], replicated
- grad_s_norm1_bias: float32 [768], replicated
- grad_s_ffn_in: float32 [768, 1536], P(None, ('head', 'seq'))
- grad_s_ffn_in_bias: float32 [1536], P(('head', 'seq'))
- grad_s_ffn_out: float32 [1536, 768], P(('head', 'seq'))
- grad_s_ffn_out_bias: float32 [768], replicated
- grad_s_norm2_gain: float32 [768], replicated
- grad_s_norm2_bias: float32 [768], replicated
Inputs may be any that keep to these rules, and one draw needn't show every extreme that they name: `lengths`: in each block of 2 consecutive sequences one sequence has length 512.
All inputs are finite; a program needn't handle non-finite values.
Results may differ from a plain program's by a relative error of at most 0.034.
Values may be sent and summed in bfloat16 or wider, within the bound.
A program may use at most 256 MiB of HBM per device.

v0:
```python
import math

import jax
import jax.numpy as jnp
from jax import lax
from jax.sharding import PartitionSpec as P

HD = 64


EPSILON = 1e-05


def layer_norm(values, gain, shift):
    center = values - jnp.mean(values, axis=-1, keepdims=True)
    spread = jnp.mean(center * center, axis=-1, keepdims=True)
    return center * lax.rsqrt(spread + EPSILON) * gain + shift


def norm_back(values, gain, shift, upstream):
    _, pull = jax.vjp(layer_norm, values, gain, shift)
    return pull(upstream)


def smooth_gate(pre):
    return 0.5 * pre * (1.0 + jnp.tanh(0.7978845608028654 * (pre + 0.044715 * pre * pre * pre)))


def gather_sequences(rows_low):
    return lax.all_gather(rows_low, "head", axis=1, tiled=True)


def head_total(partial_value):
    return lax.psum_scatter(partial_value, "head", scatter_dimension=1, tiled=True)


def gather_grads(grad_low):
    return lax.all_gather(grad_low, "head", axis=1, tiled=True)


def input_total(partial_value):
    return lax.psum_scatter(partial_value, "head", scatter_dimension=1, tiled=True)


def attention_scores(queries, keys_low, key_mask):
    scores = jnp.einsum("bqhe,bkhe->bhqk", queries, keys_low, preferred_element_type=jnp.float32)
    scores = scores * (1.0 / math.sqrt(HD))
    return jnp.where(key_mask, scores, -1000000000.0)


def attend_forward(x_query, x_keys, key_mask, w_query, b_query, w_key, w_value, b_value, w_out):
    seq_count, query_rows, model_width = x_query.shape
    key_rows = x_keys.shape[1]
    head_count = w_query.shape[1] // HD
    queries = (
        jnp.einsum("bld,dc->blc", x_query, w_query, preferred_element_type=jnp.float32) + b_query
    ).astype(jnp.bfloat16)
    keys_low = jnp.einsum("bld,dc->blc", x_keys, w_key, preferred_element_type=jnp.float32).astype(
        jnp.bfloat16
    )
    values = (
        jnp.einsum("bld,dc->blc", x_keys, w_value, preferred_element_type=jnp.float32) + b_value
    ).astype(jnp.bfloat16)
    queries = queries.reshape(seq_count, query_rows, head_count, HD)
    keys_low = keys_low.reshape(seq_count, key_rows, head_count, HD)
    values = values.reshape(seq_count, key_rows, head_count, HD)
    scores = attention_scores(queries, keys_low, key_mask)
    top_score = jnp.max(scores, axis=-1, keepdims=True)
    expo = jnp.exp(scores - top_score)
    totals = jnp.sum(expo, axis=-1, keepdims=True)
    probs = (expo / totals).astype(jnp.bfloat16)
    log_total = top_score + jnp.log(totals)
    mixed = jnp.einsum("bhqk,bkhe->bqhe", probs, values, preferred_element_type=jnp.float32)
    mixed = mixed.reshape(seq_count, query_rows, head_count * HD).astype(jnp.bfloat16)
    partial_value = jnp.einsum("blc,cd->bld", mixed, w_out, preferred_element_type=jnp.float32)
    return (partial_value, (queries, keys_low, values, mixed, log_total))


def attend_backward(x_query, x_keys, key_mask, w_query, w_key, w_value, w_out, saved, grad_out):
    queries, keys_low, values, mixed, log_total = saved
    seq_count, query_rows, head_count, head_size = queries.shape
    key_rows = keys_low.shape[1]
    scale = 1.0 / math.sqrt(HD)
    grad_wout = jnp.einsum("blc,bld->cd", mixed, grad_out, preferred_element_type=jnp.float32)
    grad_mixed = jnp.einsum(
        "bld,cd->blc", grad_out, w_out, preferred_element_type=jnp.float32
    ).astype(jnp.bfloat16)
    grad_mixed = grad_mixed.reshape(seq_count, query_rows, head_count, head_size)
    probs = jnp.exp(attention_scores(queries, keys_low, key_mask) - log_total)
    grad_probs = jnp.einsum(
        "bqhe,bkhe->bhqk", grad_mixed, values, preferred_element_type=jnp.float32
    )
    grad_values = jnp.einsum(
        "bhqk,bqhe->bkhe",
        probs.astype(jnp.bfloat16),
        grad_mixed,
        preferred_element_type=jnp.float32,
    ).astype(jnp.bfloat16)
    grad_scores = (
        probs * (grad_probs - jnp.sum(probs * grad_probs, axis=-1, keepdims=True))
    ).astype(jnp.bfloat16)
    grad_queries = (
        jnp.einsum("bhqk,bkhe->bqhe", grad_scores, keys_low, preferred_element_type=jnp.float32)
        * scale
    ).astype(jnp.bfloat16)
    grad_keys = (
        jnp.einsum("bhqk,bqhe->bkhe", grad_scores, queries, preferred_element_type=jnp.float32)
        * scale
    ).astype(jnp.bfloat16)
    grad_queries = grad_queries.reshape(seq_count, query_rows, head_count * head_size)
    grad_keys = grad_keys.reshape(seq_count, key_rows, head_count * head_size)
    grad_values = grad_values.reshape(seq_count, key_rows, head_count * head_size)
    grad_wq = jnp.einsum("bld,blc->dc", x_query, grad_queries, preferred_element_type=jnp.float32)
    grad_bq = jnp.sum(grad_queries.astype(jnp.float32), axis=(0, 1))
    grad_wk = jnp.einsum("bld,blc->dc", x_keys, grad_keys, preferred_element_type=jnp.float32)
    grad_wv = jnp.einsum("bld,blc->dc", x_keys, grad_values, preferred_element_type=jnp.float32)
    grad_bv = jnp.sum(grad_values.astype(jnp.float32), axis=(0, 1))
    back_query = jnp.einsum(
        "blc,dc->bld", grad_queries, w_query, preferred_element_type=jnp.float32
    )
    back_keys = jnp.einsum("blc,dc->bld", grad_keys, w_key, preferred_element_type=jnp.float32)
    back_keys = back_keys + jnp.einsum(
        "blc,dc->bld", grad_values, w_value, preferred_element_type=jnp.float32
    )
    return (back_query, back_keys, (grad_wq, grad_bq, grad_wk, grad_wv, grad_bv, grad_wout))


def ffn_by_tokens(rows_low, w_in, b_in, w_back):
    gathered = lax.all_gather(rows_low, ("head", "seq"), axis=0, tiled=True)
    pre = jnp.dot(gathered, w_in, preferred_element_type=jnp.float32) + b_in
    hidden = smooth_gate(pre).astype(jnp.bfloat16)
    result = lax.psum_scatter(
        jnp.dot(hidden, w_back, preferred_element_type=jnp.float32),
        ("head", "seq"),
        scatter_dimension=0,
        tiled=True,
    )
    return (result, (gathered, pre, hidden))


def ffn_back_tokens(grad_low, w_in, w_back, saved):
    gathered, pre, hidden = saved
    grads_all = lax.all_gather(grad_low, ("head", "seq"), axis=0, tiled=True)
    grad_hidden = jnp.einsum("rd,nd->rn", grads_all, w_back, preferred_element_type=jnp.float32)
    grad_back = jnp.einsum("rn,rd->nd", hidden, grads_all, preferred_element_type=jnp.float32)
    _, pull = jax.vjp(smooth_gate, pre)
    grad_pre = pull(grad_hidden)[0].astype(jnp.bfloat16)
    grad_in = jnp.einsum("rd,rn->dn", gathered, grad_pre, preferred_element_type=jnp.float32)
    grad_bias = jnp.sum(grad_pre.astype(jnp.float32), axis=0)
    grad_rows = lax.psum_scatter(
        jnp.einsum("rn,dn->rd", grad_pre, w_in, preferred_element_type=jnp.float32),
        ("head", "seq"),
        scatter_dimension=0,
        tiled=True,
    )
    return (grad_rows, (grad_in, grad_bias, grad_back))


def student_heads(s_query, s_query_bias, s_key, s_value, s_value_bias, s_attn_out, per_device):
    head_index = lax.axis_index("head")
    student_count = s_query.shape[1] // HD
    first_col = jnp.minimum(head_index * per_device, student_count - per_device) * HD
    live_mark = head_index * per_device < student_count
    col_count = per_device * HD
    slices = (
        lax.dynamic_slice_in_dim(s_query, first_col, col_count, 1),
        lax.dynamic_slice_in_dim(s_query_bias, first_col, col_count, 0),
        lax.dynamic_slice_in_dim(s_key, first_col, col_count, 1),
        lax.dynamic_slice_in_dim(s_value, first_col, col_count, 1),
        lax.dynamic_slice_in_dim(s_value_bias, first_col, col_count, 0),
        lax.dynamic_slice_in_dim(s_attn_out, first_col, col_count, 0),
    )
    return (slices, first_col, live_mark)


def place_piece(piece, like, first_col, axis_number):
    return lax.dynamic_update_slice_in_dim(
        jnp.zeros(like.shape, jnp.float32), piece, first_col, axis_number
    )


def body(
    tokens,
    lengths,
    cotangent,
    t_query,
    t_query_bias,
    t_key,
    t_value,
    t_value_bias,
    t_attn_out,
    t_attn_bias,
    t_norm1_gain,
    t_norm1_bias,
    t_ffn_in,
    t_ffn_in_bias,
    t_ffn_out,
    t_ffn_out_bias,
    t_norm2_gain,
    t_norm2_bias,
    s_query,
    s_query_bias,
    s_key,
    s_value,
    s_value_bias,
    s_attn_out,
    s_attn_bias,
    s_norm1_gain,
    s_norm1_bias,
    s_ffn_in,
    s_ffn_in_bias,
    s_ffn_out,
    s_ffn_out_bias,
    s_norm2_gain,
    s_norm2_bias,
):
    seq_count, own_rows, model_width = tokens.shape
    full_span = own_rows * lax.axis_size("head")
    positions = jnp.arange(full_span, dtype=jnp.int32)
    key_mask = (positions[None, :] < lengths[:, None])[:, None, None, :]
    whole_t = gather_sequences(tokens)
    part_t, saved_t = attend_forward(
        whole_t, whole_t, key_mask, t_query, t_query_bias, t_key, t_value, t_value_bias, t_attn_out
    )
    resid_t = tokens.astype(jnp.float32) + head_total(part_t) + t_attn_bias
    normed_t = (
        layer_norm(resid_t, t_norm1_gain, t_norm1_bias)
        .astype(jnp.bfloat16)
        .reshape(-1, model_width)
    )
    ffn_t, kept_t = ffn_by_tokens(normed_t, t_ffn_in, t_ffn_in_bias, t_ffn_out)
    summed_t = normed_t.astype(jnp.float32) + ffn_t + t_ffn_out_bias
    inputs_s = (
        layer_norm(summed_t, t_norm2_gain, t_norm2_bias)
        .astype(jnp.bfloat16)
        .reshape(seq_count, own_rows, model_width)
    )
    whole_s = gather_sequences(inputs_s)
    per_device = t_query.shape[1] // HD
    slices, first_col, live_mark = student_heads(
        s_query, s_query_bias, s_key, s_value, s_value_bias, s_attn_out, per_device
    )
    part_s, saved_s = attend_forward(
        whole_s, whole_s, key_mask, slices[0], slices[1], slices[2], slices[3], slices[4], slices[5]
    )
    attn_s = head_total(jnp.where(live_mark, part_s, 0.0))
    resid_s = inputs_s.astype(jnp.float32) + attn_s + s_attn_bias
    normed_s = (
        layer_norm(resid_s, s_norm1_gain, s_norm1_bias)
        .astype(jnp.bfloat16)
        .reshape(-1, model_width)
    )
    ffn_s, kept_s = ffn_by_tokens(normed_s, s_ffn_in, s_ffn_in_bias, s_ffn_out)
    summed_s = normed_s.astype(jnp.float32) + ffn_s + s_ffn_out_bias
    output = layer_norm(summed_s, s_norm2_gain, s_norm2_bias).reshape(
        seq_count, own_rows, model_width
    )
    upstream = cotangent.astype(jnp.float32).reshape(-1, model_width)
    grad_sum_s, grad_g2s, grad_b2s = norm_back(summed_s, s_norm2_gain, s_norm2_bias, upstream)
    grad_ffn_s = grad_sum_s.astype(jnp.bfloat16)
    grad_c2s = jnp.sum(grad_ffn_s.astype(jnp.float32), axis=0)
    grad_rows_s, ffn_grads_s = ffn_back_tokens(grad_ffn_s, s_ffn_in, s_ffn_out, kept_s)
    grad_normed_s = (grad_sum_s + grad_rows_s).reshape(seq_count, own_rows, model_width)
    grad_resid_s, grad_g1s, grad_b1s = norm_back(resid_s, s_norm1_gain, s_norm1_bias, grad_normed_s)
    grad_attn_s = grad_resid_s.astype(jnp.bfloat16)
    grad_bos = jnp.sum(grad_attn_s.astype(jnp.float32), axis=(0, 1))
    grad_whole_s = gather_grads(grad_attn_s)
    grad_whole_s = jnp.where(live_mark, grad_whole_s, jnp.zeros_like(grad_whole_s))
    back_query_s, back_keys_s, piece_grads = attend_backward(
        whole_s,
        whole_s,
        key_mask,
        slices[0],
        slices[2],
        slices[3],
        slices[5],
        saved_s,
        grad_whole_s,
    )
    grad_inputs_s = grad_resid_s + input_total(back_query_s + back_keys_s)
    attn_grads_s = (
        place_piece(piece_grads[0], s_query, first_col, 1),
        place_piece(piece_grads[1], s_query_bias, first_col, 0),
        place_piece(piece_grads[2], s_key, first_col, 1),
        place_piece(piece_grads[3], s_value, first_col, 1),
        place_piece(piece_grads[4], s_value_bias, first_col, 0),
        place_piece(piece_grads[5], s_attn_out, first_col, 0),
    )
    grad_sum_t, grad_g2t, grad_b2t = norm_back(
        summed_t, t_norm2_gain, t_norm2_bias, grad_inputs_s.reshape(-1, model_width)
    )
    grad_ffn_t = grad_sum_t.astype(jnp.bfloat16)
    grad_c2t = jnp.sum(grad_ffn_t.astype(jnp.float32), axis=0)
    grad_rows_t, ffn_grads_t = ffn_back_tokens(grad_ffn_t, t_ffn_in, t_ffn_out, kept_t)
    grad_normed_t = (grad_sum_t + grad_rows_t).reshape(seq_count, own_rows, model_width)
    grad_resid_t, grad_g1t, grad_b1t = norm_back(resid_t, t_norm1_gain, t_norm1_bias, grad_normed_t)
    grad_attn_t = grad_resid_t.astype(jnp.bfloat16)
    grad_bot = jnp.sum(grad_attn_t.astype(jnp.float32), axis=(0, 1))
    grad_whole_t = gather_grads(grad_attn_t)
    back_query_t, back_keys_t, attn_grads_t = attend_backward(
        whole_t, whole_t, key_mask, t_query, t_key, t_value, t_attn_out, saved_t, grad_whole_t
    )
    input_grad = grad_resid_t + input_total(back_query_t + back_keys_t)
    row_sums = lax.psum(
        (
            ffn_grads_t[0],
            ffn_grads_t[1],
            ffn_grads_t[2],
            ffn_grads_s[0],
            ffn_grads_s[1],
            ffn_grads_s[2],
        ),
        "row",
    )
    shard_sums = lax.psum(
        (
            attn_grads_t[0],
            attn_grads_t[1],
            attn_grads_t[2],
            attn_grads_t[3],
            attn_grads_t[4],
            attn_grads_t[5],
        ),
        ("row", "seq"),
    )
    every_sums = lax.psum(
        (
            attn_grads_s[0],
            attn_grads_s[1],
            attn_grads_s[2],
            attn_grads_s[3],
            attn_grads_s[4],
            attn_grads_s[5],
            grad_bot,
            grad_g1t,
            grad_b1t,
            grad_c2t,
            grad_g2t,
            grad_b2t,
            grad_bos,
            grad_g1s,
            grad_b1s,
            grad_c2s,
            grad_g2s,
            grad_b2s,
        ),
        ("row", "head", "seq"),
    )
    return (
        output,
        input_grad,
        shard_sums[0],
        shard_sums[1],
        shard_sums[2],
        shard_sums[3],
        shard_sums[4],
        shard_sums[5],
        every_sums[6],
        every_sums[7],
        every_sums[8],
        row_sums[0],
        row_sums[1],
        row_sums[2],
        every_sums[9],
        every_sums[10],
        every_sums[11],
        every_sums[0],
        every_sums[1],
        every_sums[2],
        every_sums[3],
        every_sums[4],
        every_sums[5],
        every_sums[12],
        every_sums[13],
        every_sums[14],
        row_sums[3],
        row_sums[4],
        row_sums[5],
        every_sums[15],
        every_sums[16],
        every_sums[17],
    )


def solution(mesh):
    in_specs = (
        P(("row", "seq"), "head", None),
        P(("row", "seq")),
        P(("row", "seq"), "head", None),
        P(None, "head"),
        P("head"),
        P(None, "head"),
        P(None, "head"),
        P("head"),
        P("head", None),
        P(),
        P(),
        P(),
        P(None, ("head", "seq")),
        P(("head", "seq")),
        P(("head", "seq"), None),
        P(),
        P(),
        P(),
        P(),
        P(),
        P(),
        P(),
        P(),
        P(),
        P(),
        P(),
        P(),
        P(None, ("head", "seq")),
        P(("head", "seq")),
        P(("head", "seq"), None),
        P(),
        P(),
        P(),
    )
    out_specs = (
        P(("row", "seq"), "head", None),
        P(("row", "seq"), "head", None),
        P(None, "head"),
        P("head"),
        P(None, "head"),
        P(None, "head"),
        P("head"),
        P("head", None),
        P(),
        P(),
        P(),
        P(None, ("head", "seq")),
        P(("head", "seq")),
        P(("head", "seq"), None),
        P(),
        P(),
        P(),
        P(),
        P(),
        P(),
        P(),
        P(),
        P(),
        P(),
        P(),
        P(),
        P(None, ("head", "seq")),
        P(("head", "seq")),
        P(("head", "seq"), None),
        P(),
        P(),
        P(),
    )
    return jax.shard_map(body, mesh=mesh, in_specs=in_specs, out_specs=out_specs, check_vma=False)
```

profile of v0, /device:TPU:0, one launch (start us, length us, event | category | flops | bytes accessed | tf_op | source)
XLA Modules:
  0.0 1309.3 jit_solution(1234836153722084233)
XLA Ops:
  8.7 40.7 %all-gather.9.cloned.1.call-done = bf16[2,512,768]{2,1,0:T(8,128)(2,1)} async-done(((bf16[2,128,768]{2,1,0:T(8,128)(2,1)}), bf16[2,512,768]{2,1,0:T(8,128)(2,1)}) %all-gather.9.cloned.1.call-update) | async-done | bytes 1572880 | tf_op jit(solution)/shard_map/all_gather | solution.py:30
  60.3 2.3 fusion.69
  62.7 59.2 %reduce-scatter.9.cloned.1.call-done = f32[2,128,768]{2,1,0:T(8,128)} async-done(((f32[2,512,768]{2,1,0:T(8,128)}), f32[2,128,768]{2,1,0:T(8,128)}) %reduce-scatter.9.cloned.1.call-update) | async-done | bytes 786448 | tf_op jit(solution)/shard_map/reduce_scatter | solution.py:34
  124.6 38.4 %all-gather.11.cloned.1.call-done = bf16[2048,768]{1,0:T(8,128)(2,1)} async-done(((bf16[256,768]{1,0:T(8,128)(2,1)}), bf16[2048,768]{1,0:T(8,128)(2,1)}) %all-gather.11.cloned.1.call-update) | async-done | bytes 3145744 | tf_op jit(solution)/shard_map/all_gather | solution.py:129
  163.0 3.7 convolution_add_fusion
  168.5 5.0 fusion.98
  173.6 68.7 %reduce-scatter.11.cloned.1.call-done = f32[256,768]{1,0:T(8,128)} async-done(((f32[2048,768]{1,0:T(8,128)}), f32[256,768]{1,0:T(8,128)}) %reduce-scatter.11.cloned.1.call-update) | async-done | bytes 786448 | tf_op jit(solution)/shard_map/reduce_scatter | solution.py:132
  246.2 34.9 %all-gather.13.cloned.1.call-done = bf16[2,512,768]{2,1,0:T(8,128)(2,1)} async-done(((bf16[2,128,768]{2,1,0:T(8,128)(2,1)}), bf16[2,512,768]{2,1,0:T(8,128)(2,1)}) %all-gather.13.cloned.1.call-update) | async-done | bytes 1572880 | tf_op jit(solution)/shard_map/all_gather | solution.py:30
  295.5 59.2 %reduce-scatter.13.cloned.1.call-done = f32[2,128,768]{2,1,0:T(8,128)} async-done(((f32[2,512,768]{2,1,0:T(8,128)}), f32[2,128,768]{2,1,0:T(8,128)}) %reduce-scatter.13.cloned.1.call-update) | async-done | bytes 786448 | tf_op jit(solution)/shard_map/reduce_scatter | solution.py:34
  358.1 38.4 %all-gather.15.cloned.1.call-done = bf16[2048,768]{1,0:T(8,128)(2,1)} async-done(((bf16[256,768]{1,0:T(8,128)(2,1)}), bf16[2048,768]{1,0:T(8,128)(2,1)}) %all-gather.15.cloned.1.call-update) | async-done | bytes 3145744 | tf_op jit(solution)/shard_map/all_gather | solution.py:129
  396.5 3.1 convolution_add_fusion.1
  400.8 4.0 fusion.96
  404.8 68.8 %reduce-scatter.15.cloned.1.call-done = f32[256,768]{1,0:T(8,128)} async-done(((f32[2048,768]{1,0:T(8,128)}), f32[256,768]{1,0:T(8,128)}) %reduce-scatter.15.cloned.1.call-update) | async-done | bytes 786448 | tf_op jit(solution)/shard_map/reduce_scatter | solution.py:132
  481.0 36.7 %all-gather.17.cloned.1.call-done = bf16[2048,768]{1,0:T(8,128)(2,1)} async-done(((bf16[256,768]{1,0:T(8,128)(2,1)}), bf16[2048,768]{1,0:T(8,128)(2,1)}) %all-gather.17.cloned.1.call-update) | async-done | bytes 3145744 | tf_op jit(solution)/shard_map/all_gather | solution.py:143
  517.7 5.2 convert_reduce_fusion.1
  523.8 3.6 fusion.112
  527.7 68.6 %reduce-scatter.17.cloned.1.call-done = f32[256,768]{1,0:T(8,128)} async-done(((f32[2048,768]{1,0:T(8,128)}), f32[256,768]{1,0:T(8,128)}) %reduce-scatter.17.cloned.1.call-update) | async-done | bytes 786448 | tf_op jit(solution)/shard_map/reduce_scatter | solution.py:150
  603.2 3.0 convert_reduce_fusion.4
  606.3 35.5 %all-gather.19.cloned.1.call-done = bf16[2,512,768]{2,1,0:T(8,128)(2,1)} async-done(((bf16[2,128,768]{2,1,0:T(8,128)(2,1)}), bf16[2,512,768]{2,1,0:T(8,128)(2,1)}) %all-gather.19.cloned.1.call-update) | async-done | bytes 1572880 | tf_op jit(solution)/shard_map/all_gather | solution.py:38
  644.0 5.4 convert_reduce_fusion.5
  649.3 4.3 multiply_reduce_fusion.1
  660.7 2.5 add_add_fusion.1
  663.3 58.8 %reduce-scatter.19.cloned.1.call-done = f32[2,128,768]{2,1,0:T(8,128)} async-done(((f32[2,512,768]{2,1,0:T(8,128)}), f32[2,128,768]{2,1,0:T(8,128)}) %reduce-scatter.19.cloned.1.call-update) | async-done | bytes 786448 | tf_op jit(solution)/shard_map/reduce_scatter | solution.py:42
  722.1 2.6 fusion.102
  728.6 38.2 %all-gather.21.cloned.1.call-done = bf16[2048,768]{1,0:T(8,128)(2,1)} async-done(((bf16[256,768]{1,0:T(8,128)(2,1)}), bf16[2048,768]{1,0:T(8,128)(2,1)}) %all-gather.21.cloned.1.call-update) | async-done | bytes 3145744 | tf_op jit(solution)/shard_map/all_gather | solution.py:143
  766.8 7.3 convert_reduce_fusion
  775.2 4.5 fusion.113
  779.8 68.8 %reduce-scatter.21.cloned.1.call-done = f32[256,768]{1,0:T(8,128)} async-done(((f32[2048,768]{1,0:T(8,128)}), f32[256,768]{1,0:T(8,128)}) %reduce-scatter.21.cloned.1.call-update) | async-done | bytes 786448 | tf_op jit(solution)/shard_map/reduce_scatter | solution.py:150
  855.7 35.5 %all-gather.23.cloned.1.call-done = bf16[2,512,768]{2,1,0:T(8,128)(2,1)} async-done(((bf16[2,128,768]{2,1,0:T(8,128)(2,1)}), bf16[2,512,768]{2,1,0:T(8,128)(2,1)}) %all-gather.23.cloned.1.call-update) | async-done | bytes 1572880 | tf_op jit(solution)/shard_map/all_gather | solution.py:38
  893.3 4.1 convert_reduce_fusion.9
  897.4 4.3 multiply_reduce_fusion
  909.4 2.5 convolution_bitcast_fusion
  912.9 4.8 dynamic_update_slice.21
  917.7 2.5 convolution_bitcast_fusion.1
  921.3 4.7 dynamic_update_slice.20
  926.1 2.5 convolution_bitcast_fusion.2
  929.7 4.7 dynamic_update_slice.18
  937.5 3.8 fusion.115
  941.4 3.9 fusion.95
  945.3 2.8 fusion.114
  948.1 2.6 fusion.97
  950.8 2.9 convolution_bitcast_fusion.3
  958.5 10.4 all-reduce.4
  968.9 40.4 %all-reduce = (f32[768]{0:T(1024)}, f32[768]{0:T(1024)}, f32[768]{0:T(1024)}, f32[768]{0:T(1024)}, f32[768]{0:T(1024)}, /*index=5*/f32[768]{0:T(1024)}, f32[384]...) all-reduce(f32[768]{0:T(1024)S(1)} %get-tuple-element.86, ...), channel_id=1, replica_groups=mesh['row'=4,'head'=4,'seq'=2] {'row','head','seq'}, use_global_device_ids=true, to_apply=%region_39.40 | all-reduce | flops 9984 | bytes 79872 | tf_op jit(solution)/shard_map/psum | solution.py:326
  1009.5 13.2 %all-reduce.2 = (f32[192]{0:T(256)}, f32[192]{0:T(256)}) all-reduce(f32[192]{0:T(256)S(1)} %reduce_sum.384, f32[192]{0:T(256)S(1)} %reduce_sum.386), channel_id=1, replica_groups=mesh['row'=4,'head'=4,'seq'=2] {'row','seq'}, use_global_device_ids=true, to_apply=%region_32.33 | all-reduce | flops 384 | bytes 3072 | tf_op jit(solution)/shard_map/psum | solution.py:315
  1024.9 96.1 %all-reduce.10.cloned.1.call-done = (f32[768,384]{1,0:T(8,128)}, f32[768,384]{1,0:T(8,128)}, f32[768,384]{1,0:T(8,128)}, f32[384,768]{1,0:T(8,128)}) async-done(((f32[768,384]{1,0:T(8,128)}, f32[768,384]{1,0:T(8,128)}, f32[768,384]{1,0:T(8,128)}, f32[384,768]{1,0:T(8,128)}), (f32[768,384]{1,0:T(8,128)}, f32[768,384]{1,0:T(8,128)}, f32[768,384]{1,0:T(8,128)}, ...) | async-done | bytes 4718608 | tf_op jit(solution)/shard_map/psum | solution.py:326
  1121.0 98.4 %all-reduce.14.cloned.1.call-done = (f32[768,384]{1,0:T(8,128)}, f32[384,768]{1,0:T(8,128)}, f32[768,192]{0,1:T(8,128)}, f32[192,768]{1,0:T(8,128)}) async-done(((f32[768,384]{1,0:T(8,128)}, f32[384,768]{1,0:T(8,128)}, f32[768,192]{0,1:T(8,128)}, f32[192,768]{1,0:T(8,128)}), (f32[768,384]{1,0:T(8,128)}, f32[384,768]{1,0:T(8,128)}, f32[768,192]{0,1:T(8,128)}, ...) | async-done | bytes 3538960 | tf_op jit(solution)/shard_map/psum | solution.py:304
  1219.4 68.4 %all-reduce.12.cloned.1.call-done = (f32[768,192]{0,1:T(8,128)}, f32[768,192]{0,1:T(8,128)}, f32[768,192]{0,1:T(8,128)}, f32[192,768]{1,0:T(8,128)}) async-done(((f32[768,192]{0,1:T(8,128)}, f32[768,192]{0,1:T(8,128)}, f32[768,192]{0,1:T(8,128)}, f32[192,768]{1,0:T(8,128)}), (f32[768,192]{0,1:T(8,128)}, f32[768,192]{0,1:T(8,128)}, f32[768,192]{0,1:T(8,128)}, ...) | async-done | bytes 2359312 | tf_op jit(solution)/shard_map/psum | solution.py:315
  (382 shorter events, 113.2 us)
Async XLA Ops:
  7.2 161.3 %copy-start = (bf16[384,768]{1,0:T(8,128)(2,1)S(1)}, bf16[384,768]{1,0:T(8,128)(2,1)}, u32[]{:S(2)}) copy-start(bf16[384,768]{1,0:T(8,128)(2,1)} %param.47) | copy-start | bytes 1769476
  7.2 42.2 %all-gather.9.cloned.1.call-start = ((), (), s32[]{:S(2)}) async-start(), calls=%async_computation.8 | async-start | bytes 1966080 | tf_op jit(solution)/shard_map/all_gather | solution.py:30
  8.0 114.0 %reduce-scatter.9.cloned.1.call-start = ((), (), s32[]{:S(2)}) async-start(), calls=%async_computation.9 | async-start | bytes 3932160 | tf_op jit(solution)/shard_map/reduce_scatter | solution.py:34
  60.2 61.7 %copy-start.38 = (bf16[2,128,768]{2,1,0:T(8,128)(2,1)S(1)}, bf16[2,128,768]{2,1,0:T(8,128)(2,1)}, u32[]{:S(2)}) copy-start(bf16[2,128,768]{2,1,0:T(8,128)(2,1)} %param.33) | copy-start | bytes 1179652
  60.3 61.7 %copy-start.96 = (f32[768]{0:T(1024)S(1)}, f32[768]{0:T(1024)}, u32[]{:S(2)}) copy-start(f32[768]{0:T(1024)} %param.42) | copy-start | bytes 9220
  62.6 60.9 %copy-start.72 = (f32[768]{0:T(1024)S(1)}, f32[768]{0:T(1024)}, u32[]{:S(2)}) copy-start(f32[768]{0:T(1024)} %param.43) | copy-start | bytes 9220
  62.6 60.9 %copy-start.97 = (f32[768]{0:T(1024)S(1)}, f32[768]{0:T(1024)}, u32[]{:S(2)}) copy-start(f32[768]{0:T(1024)} %param.44) | copy-start | bytes 9220
  62.6 62.0 %copy-start.105 = (bf16[384]{0:T(512)(128)(2,1)S(1)}, bf16[384]{0:T(512)(128)(2,1)}, u32[]{:S(2)}) copy-start(bf16[384]{0:T(512)(128)(2,1)} %param.46) | copy-start | bytes 2308
  62.6 100.4 %copy-start.54 = (bf16[768,384]{1,0:T(8,128)(2,1)S(1)}, bf16[768,384]{1,0:T(8,128)(2,1)}, u32[]{:S(2)}) copy-start(bf16[768,384]{1,0:T(8,128)(2,1)} %param.45) | copy-start | bytes 1769476
  62.7 100.3 %all-gather.11.cloned.1.call-start = ((), (), s32[]{:S(2)}) async-start(), calls=%async_computation.10 | async-start | bytes 3538944 | tf_op jit(solution)/shard_map/all_gather | solution.py:129
  124.5 117.8 %reduce-scatter.11.cloned.1.call-start = ((), (), s32[]{:S(2)}) async-start(), calls=%async_computation.11 | async-start | bytes 7077888 | tf_op jit(solution)/shard_map/reduce_scatter | solution.py:132
  173.5 68.9 %copy-start.25 = (bf16[2,128,768]{2,1,0:T(8,128)(2,1)S(1)}, bf16[2,128,768]{2,1,0:T(8,128)(2,1)}, u32[]{:S(2)}) copy-start(bf16[2,128,768]{2,1,0:T(8,128)(2,1)} %add_convert_fusion.2) | copy-start | bytes 1179652
  173.5 68.9 %copy-start.98 = (f32[768]{0:T(1024)S(1)}, f32[768]{0:T(1024)}, u32[]{:S(2)}) copy-start(f32[768]{0:T(1024)} %param.48) | copy-start | bytes 9220
  173.5 71.1 %copy-start.80 = (f32[768]{0:T(1024)S(1)}, f32[768]{0:T(1024)}, u32[]{:S(2)}) copy-start(f32[768]{0:T(1024)} %param.49) | copy-start | bytes 9220
  173.5 71.1 %copy-start.99 = (f32[768]{0:T(1024)S(1)}, f32[768]{0:T(1024)}, u32[]{:S(2)}) copy-start(f32[768]{0:T(1024)} %param.50) | copy-start | bytes 9220
  173.5 72.5 %copy-start.107 = (f32[384]{0:T(512)S(1)}, f32[384]{0:T(512)}, u32[]{:S(2)}) copy-start(f32[384]{0:T(512)} %param.52) | copy-start | bytes 4612
  173.5 72.6 %copy-start.108 = (f32[384]{0:T(512)S(1)}, f32[384]{0:T(512)}, u32[]{:S(2)}) copy-start(f32[384]{0:T(512)} %param.55) | copy-start | bytes 4612
  173.5 107.6 %copy-start.50 = (bf16[768,384]{1,0:T(8,128)(2,1)S(1)}, bf16[768,384]{1,0:T(8,128)(2,1)}, u32[]{:S(2)}) copy-start(bf16[768,384]{1,0:T(8,128)(2,1)} %param.53) | copy-start | bytes 1769476
  173.5 109.8 %copy-start.52 = (bf16[768,384]{1,0:T(8,128)(2,1)S(1)}, bf16[768,384]{1,0:T(8,128)(2,1)}, u32[]{:S(2)}) copy-start(bf16[768,384]{1,0:T(8,128)(2,1)} %param.51) | copy-start | bytes 1769476
  173.5 107.6 %all-gather.13.cloned.1.call-start = ((), (), s32[]{:S(2)}) async-start(), calls=%async_computation.12 | async-start | bytes 1966080 | tf_op jit(solution)/shard_map/all_gather | solution.py:30
  245.5 109.2 %reduce-scatter.13.cloned.1.call-start = ((), (), s32[]{:S(2)}) async-start(), calls=%async_computation.13 | async-start | bytes 3932160 | tf_op jit(solution)/shard_map/reduce_scatter | solution.py:34
  293.2 61.6 %copy-start.100 = (f32[768]{0:T(1024)S(1)}, f32[768]{0:T(1024)}, u32[]{:S(2)}) copy-start(f32[768]{0:T(1024)} %param.57) | copy-start | bytes 9220
  295.4 61.6 %copy-start.71 = (f32[768]{0:T(1024)S(1)}, f32[768]{0:T(1024)}, u32[]{:S(2)}) copy-start(f32[768]{0:T(1024)} %param.58) | copy-start | bytes 9220
  295.4 61.6 %copy-start.101 = (f32[768]{0:T(1024)S(1)}, f32[768]{0:T(1024)}, u32[]{:S(2)}) copy-start(f32[768]{0:T(1024)} %param.59) | copy-start | bytes 9220
  295.4 62.6 %copy-start.111 = (bf16[192]{0:T(256)(128)(2,1)S(1)}, bf16[192]{0:T(256)(128)(2,1)}, u32[]{:S(2)}) copy-start(bf16[192]{0:T(256)(128)(2,1)} %param.61) | copy-start | bytes 1156
  295.5 101.0 %all-gather.15.cloned.1.call-start = ((), (), s32[]{:S(2)}) async-start(), calls=%async_computation.14 | async-start | bytes 3538944 | tf_op jit(solution)/shard_map/all_gather | solution.py:129
  358.0 115.6 %reduce-scatter.15.cloned.1.call-start = ((), (), s32[]{:S(2)}) async-start(), calls=%async_computation.15 | async-start | bytes 7077888 | tf_op jit(solution)/shard_map/reduce_scatter | solution.py:132
  404.8 68.9 %copy-start.102 = (f32[768]{0:T(1024)S(1)}, f32[768]{0:T(1024)}, u32[]{:S(2)}) copy-start(f32[768]{0:T(1024)} %param.63) | copy-start | bytes 9220
  404.8 70.6 %copy-start.81 = (f32[768]{0:T(1024)S(1)}, f32[768]{0:T(1024)}, u32[]{:S(2)}) copy-start(f32[768]{0:T(1024)} %param.64) | copy-start | bytes 9220
  404.8 72.5 %copy-start.103 = (f32[768]{0:T(1024)S(1)}, f32[768]{0:T(1024)}, u32[]{:S(2)}) copy-start(f32[768]{0:T(1024)} %param.65) | copy-start | bytes 9220
  404.8 112.9 %all-gather.17.cloned.1.call-start = ((), (), s32[]{:S(2)}) async-start(), calls=%async_computation.16 | async-start | bytes 3538944 | tf_op jit(solution)/shard_map/all_gather | solution.py:143
  480.9 115.4 %reduce-scatter.17.cloned.1.call-start = ((), (), s32[]{:S(2)}) async-start(), calls=%async_computation.17 | async-start | bytes 7077888 | tf_op jit(solution)/shard_map/reduce_scatter | solution.py:150
  527.5 114.4 %all-gather.19.cloned.1.call-start = ((), (), s32[]{:S(2)}) async-start(), calls=%async_computation.18 | async-start | bytes 1966080 | tf_op jit(solution)/shard_map/all_gather | solution.py:38
  606.2 115.9 %reduce-scatter.19.cloned.1.call-start = ((), (), s32[]{:S(2)}) async-start(), calls=%async_computation.19 | async-start | bytes 3932160 | tf_op jit(solution)/shard_map/reduce_scatter | solution.py:42
  663.3 103.5 %all-gather.21.cloned.1.call-start = ((), (), s32[]{:S(2)}) async-start(), calls=%async_computation.20 | async-start | bytes 3538944 | tf_op jit(solution)/shard_map/all_gather | solution.py:143
  728.3 120.3 %reduce-scatter.21.cloned.1.call-start = ((), (), s32[]{:S(2)}) async-start(), calls=%async_computation.21 | async-start | bytes 7077888 | tf_op jit(solution)/shard_map/reduce_scatter | solution.py:150
  779.7 68.9 %copy-start.93 = (f32[256]{0:T(256)S(1)}, f32[256]{0:T(256)}, u32[]{:S(2)}) copy-start(f32[256]{0:T(256)} %copy-done.92) | copy-start | bytes 3076
  779.7 70.4 %copy-start.73 = (f32[768]{0:T(1024)S(1)}, f32[768]{0:T(1024)}, u32[]{:S(2)}) copy-start(f32[768]{0:T(1024)} %param.43) | copy-start | bytes 9220
  779.7 70.4 %copy-start.77 = (f32[2,128]{1,0:T(2,128)S(1)}, f32[2,128]{1,0:T(2,128)}, u32[]{:S(2)}) copy-start(f32[2,128]{1,0:T(2,128)} %copy-done.76) | copy-start | bytes 3076
  779.7 70.4 %copy-start.79 = (f32[2,128]{1,0:T(2,128)S(1)}, f32[2,128]{1,0:T(2,128)}, u32[]{:S(2)}) copy-start(f32[2,128]{1,0:T(2,128)} %copy-done.78) | copy-start | bytes 3076
  779.8 70.8 %copy-start.91 = (f32[2,128]{1,0:T(2,128)S(1)}, f32[2,128]{1,0:T(2,128)}, u32[]{:S(2)}) copy-start(f32[2,128]{1,0:T(2,128)} %copy-done.90) | copy-start | bytes 3076
  779.8 111.4 %all-gather.23.cloned.1.call-start = ((), (), s32[]{:S(2)}) async-start(), calls=%async_computation.22 | async-start | bytes 1966080 | tf_op jit(solution)/shard_map/all_gather | solution.py:38
  855.6 167.1 %reduce-scatter.23.cloned.1.call-start = ((), (), s32[]{:S(2)}) async-start(), calls=%async_computation.23 | async-start | bytes 3932160 | tf_op jit(solution)/shard_map/reduce_scatter | solution.py:42
  909.1 211.9 %all-reduce.10.cloned.1.call-start = ((), (), s32[]{:S(2)}) async-start(), calls=%async_computation.24 | async-start | bytes 9437184 | tf_op jit(solution)/shard_map/psum | solution.py:326
  937.5 281.9 %all-reduce.14.cloned.1.call-start = ((), (), s32[]{:S(2)}) async-start(), calls=%async_computation.26 | async-start | bytes 7077888 | tf_op jit(solution)/shard_map/psum | solution.py:304
  950.7 337.1 %all-reduce.12.cloned.1.call-start = ((), (), s32[]{:S(2)}) async-start(), calls=%async_computation.25 | async-start | bytes 4718592 | tf_op jit(solution)/shard_map/psum | solution.py:315
  956.5 66.2 %copy-start.8 = (f32[256,768]{1,0:T(8,128)S(1)}, f32[256,768]{1,0:T(8,128)}, u32[]{:S(2)}) copy-start(f32[256,768]{1,0:T(8,128)} %copy-done.7) | copy-start | bytes 2359300
  1219.4 75.2 %copy-start.47 = (f32[768,384]{1,0:T(8,128)S(1)}, f32[768,384]{1,0:T(8,128)}, u32[]{:S(2)}) copy-start(f32[768,384]{1,0:T(8,128)} %get-tuple-element.128) | copy-start | bytes 3538948
  (89 other events, 536.1 us)
Sparse Core Ops, SparseCore 0:
  9.6 39.7 all-gather.8
  62.8 59.1 reduce-scatter.8
  124.6 38.2 all-gather.10
  173.6 68.6 reduce-scatter.10
  245.6 35.4 all-gather.12
  295.6 59.1 reduce-scatter.12
  358.1 38.2 all-gather.14
  404.9 68.6 reduce-scatter.14
  481.1 36.6 all-gather.16
  527.6 68.6 reduce-scatter.16
  606.4 35.4 all-gather.18
  663.4 58.6 reduce-scatter.18
  728.4 38.2 all-gather.20
  779.9 68.6 reduce-scatter.20
  855.7 35.4 all-gather.22
  909.2 59.0 reduce-scatter.22
  975.4 145.5 all-reduce.9
  1125.9 93.4 all-reduce.13
  1224.4 63.3 all-reduce.11
where the time goes:
time: 1320 us; the launch traced here: 1310 us
  waiting for transfers between devices  1010 us (77%)
  matrix products  122 us (9%)
  blocking collectives  64 us (5%)
  local copies, waits for them, and re-layouts  47.7 us (4%)
  other arithmetic  44.1 us (3%)
  between operations  15.8 us (1%)
    reduce_scatter x2, waiting for transfers between devices, ffn_by_tokens(): lax.psum_scatter(jnp.dot(hidden, w_back, preferred_element_type=jnp.float...  138 us
    reduce_scatter x2, waiting for transfers between devices, ffn_back_tokens(): lax.psum_scatter(jnp.einsum('rn,dn->rd', grad_pre, w_in, preferred_elemen...  137 us
    reduce_scatter x2, waiting for transfers between devices, head_total(): lax.psum_scatter(partial_value, 'head', scatter_dimension=1, tiled=True)  118 us
    psum x1, waiting for transfers between devices, body(): lax.psum((ffn_grads_t[0], ffn_grads_t[1], ffn_grads_t[2], ffn_grads_s[0],...  98.4 us
    psum x1, waiting for transfers between devices, body(): lax.psum((attn_grads_s[0], attn_grads_s[1], attn_grads_s[2], attn_grads_s...  96.1 us
    all_gather x2, waiting for transfers between devices, ffn_by_tokens(): gathered = lax.all_gather(rows_low, ('head', 'seq'), axis=0, tiled=True)  76.8 us
    all_gather x2, waiting for transfers between devices, gather_sequences(): return lax.all_gather(rows_low, 'head', axis=1, tiled=True)  75.6 us
    all_gather x2, waiting for transfers between devices, ffn_back_tokens(): grads_all = lax.all_gather(grad_low, ('head', 'seq'), axis=0, tiled=True)  74.9 us
  transfers between devices with their start and end apart: 19, of which 18 were waited for; matrix products, arithmetic and copies ran while one was open for 4% of the time, Pallas kernels for 0%

commit v1 on v0

v1 whole, which is shorter than its diff:
```python
import functools

import jax
import jax.numpy as jnp
from jax import lax
from jax.experimental import pallas as pl
from jax.experimental.pallas import tpu as pltpu
from jax.sharding import PartitionSpec as P

MESH = pl.DeviceIdType.MESH
F32 = jnp.float32
BF = jnp.bfloat16
EPS = 1e-5
MASKED = -1000000000.0
VMEM_LIMIT = 63 << 20


class Place:
    def __init__(self):
        self.r = lax.axis_index("row")
        self.z = lax.axis_index("head")
        self.s = lax.axis_index("seq")
        self.c = lax.rem(self.s, 2)

    def core(self):
        return (self.r, self.z, self.s + 1 - 2 * self.c)

    def line_index(self, step):
        return lax.rem(self.z + step + 4, 4)

    def line(self, step):
        return (self.r, self.line_index(step), self.s)

    def plane_index(self, k):
        if k == 1:
            return self.r + 1 - 2 * lax.rem(self.r, 2)
        if k == 2:
            return lax.rem(self.r + 2, 4)
        return 3 - self.r

    def plane(self, k):
        return (self.plane_index(k), self.z, self.s)


def greet(me):
    barrier = pltpu.get_barrier_semaphore()
    others = [me.core()] + [me.line(i) for i in (1, 2, 3)] + [me.plane(k) for k in (1, 2, 3)]
    for other in others:
        pl.semaphore_signal(barrier, inc=1, device_id=other, device_id_type=MESH)
    pl.semaphore_wait(barrier, len(others))


def remote(src, dst, send_sem, recv_sem, device):
    return pltpu.make_async_remote_copy(
        src_ref=src, dst_ref=dst, send_sem=send_sem, recv_sem=recv_sem, device_id=device, device_id_type=MESH
    )


def rows_of(index, count):
    return pl.ds(pl.multiple_of(index * count, 16), count)


def gather_kernel(*refs):
    me = Place()
    r, z, s, c = me.r, me.z, me.s, me.c
    (tok, cot, lens, pack, tq, tk, tv, to, ti, tf, si, sf) = refs[:12]
    (X, CT, LN, BP, WQ, WK, WV, WO, WI, WF, SI, SF) = refs[12:24]
    (zs, zr, ps, pr, ls, xs, xr, fs, fr) = refs[24:]
    greet(me)
    owner = z // 2 == c

    seqs = [(tok, X), (cot, CT)]
    for a, (src, dst) in enumerate(seqs):
        for j in range(2):
            target = 2 * c + j

            @pl.when(target != z)
            def _():
                remote(src.at[j], dst.at[z], xs.at[a, j], xr.at[a, z], (r, target, s)).start()

            @pl.when(target == z)
            def _():
                pltpu.make_async_copy(src.at[j], dst.at[z], xr.at[a, z]).start()

    shards = [(tq, WQ, 2), (tk, WK, 2), (tv, WV, 2), (to, WO, 2), (ti, WI, 4), (tf, WF, 4), (si, SI, 4), (sf, SF, 4)]

    def when_unit(count, cond):
        return (lambda f: pl.when(cond)(f)) if count == 2 else (lambda f: f())

    for w, (src, dst, count) in enumerate(shards):
        piece = rows_of(r, src.shape[0] // 4)
        slot = z % 2 if count == 2 else z

        @when_unit(count, owner)
        def _():
            pltpu.make_async_copy(src, dst.at[slot], ls.at[w]).start()
            for d in (1, 2, 3):
                remote(src.at[piece], dst.at[slot, piece], zs.at[w, d - 1], zr.at[w, d - 1], me.line(d)).start()

    own_pack = pltpu.make_async_copy(pack, BP.at[z], ls.at[8])
    own_pack.start()
    for d in (1, 2, 3):
        remote(pack, BP.at[z], zs.at[8, d - 1], zr.at[8, d - 1], me.line(d)).start()

    @pl.when(owner)
    def _():
        mine = pltpu.make_async_copy(lens.at[z % 2], LN, ls.at[9])
        mine.start()
        remote(lens.at[z % 2], LN, fs.at[2, 0], fr.at[2, 0], me.core()).start()
        for a, (src, dst) in enumerate(seqs):
            pltpu.make_async_copy(src.at[0], dst.at[z], xr.at[a, z]).wait()
            remote(dst.at[z], dst.at[z], fs.at[a, 0], fr.at[a, z], me.core()).start()
            for d in (1, 2, 3):
                frm = me.line_index(-d)
                remote(src.at[0], dst.at[frm], xs.at[a, 0], xr.at[a, frm], me.core()).wait_recv()
                remote(dst.at[frm], dst.at[frm], fs.at[a, d], fr.at[a, frm], me.core()).start()
        mine.wait()

    for w, (src, dst, count) in enumerate(shards):
        piece = rows_of(r, src.shape[0] // 4)
        for d in (1, 2, 3):
            frm = me.line_index(-d)
            slot = frm % 2 if count == 2 else frm

            @when_unit(count, frm // 2 == c)
            def _():
                part = dst.at[slot, piece]
                remote(part, part, zs.at[w, d - 1], zr.at[w, d - 1], me.core()).wait_recv()
                for k in (1, 2, 3):
                    remote(part, part, ps.at[w, d - 1, k - 1], pr.at[w, d - 1, k - 1], me.plane(k)).start()

    for w, (src, dst, count) in enumerate(shards):
        piece = rows_of(r, src.shape[0] // 4)
        slot_own = z % 2 if count == 2 else z

        @when_unit(count, owner)
        def _():
            pltpu.make_async_copy(src, dst.at[slot_own], ls.at[w]).wait()
            for d in (1, 2, 3):
                remote(src.at[piece], dst.at[slot_own, piece], zs.at[w, d - 1], zr.at[w, d - 1], me.line(d)).wait_send()

        for d in (1, 2, 3):
            frm = me.line_index(-d)
            slot = frm % 2 if count == 2 else frm

            @when_unit(count, frm // 2 == c)
            def _():
                for k in (1, 2, 3):
                    theirs = dst.at[slot, rows_of(me.plane_index(k), src.shape[0] // 4)]
                    remote(theirs, theirs, ps.at[w, d - 1, k - 1], pr.at[w, d - 1, k - 1], me.plane(k)).wait()

    own_pack.wait()
    for d in (1, 2, 3):
        remote(pack, BP.at[me.line_index(-d)], zs.at[8, d - 1], zr.at[8, d - 1], me.line(d)).wait()
    for a, (src, dst) in enumerate(seqs):
        for j in range(2):

            @pl.when(2 * c + j != z)
            def _():
                remote(src.at[j], dst.at[z], xs.at[a, j], xr.at[a, z], me.core()).wait_send()

    @pl.when(owner)
    def _():
        remote(lens.at[0], LN, fs.at[2, 0], fr.at[2, 0], me.core()).wait_send()
        for a, (src, dst) in enumerate(seqs):
            for d in range(4):
                remote(dst.at[0], dst.at[0], fs.at[a, d], fr.at[a, 0], me.core()).wait_send()

    @pl.when(jnp.logical_not(owner))
    def _():
        remote(lens.at[0], LN, fs.at[2, 0], fr.at[2, 0], me.core()).wait_recv()
        for a, (src, dst) in enumerate(seqs):
            for d in range(4):
                remote(dst.at[d], dst.at[d], fs.at[a, d], fr.at[a, d], me.core()).wait_recv()


def nn(a, b):
    return lax.dot_general(a, b, (((1,), (0,)), ((), ())), preferred_element_type=F32)


def nt(a, b):
    return lax.dot_general(a, b, (((1,), (1,)), ((), ())), preferred_element_type=F32)


def tn(a, b):
    return lax.dot_general(a, b, (((0,), (0,)), ((), ())), preferred_element_type=F32)


def norm_parts(value):
    center = value - jnp.mean(value, axis=-1, keepdims=True)
    spread = jnp.mean(center * center, axis=-1, keepdims=True)
    rstd = lax.rsqrt(spread + EPS)
    return center * rstd, rstd


def norm_grad(xh, rstd, gain, dy):
    scaled = dy * gain
    mean_one = jnp.mean(scaled, axis=-1, keepdims=True)
    mean_two = jnp.mean(scaled * xh, axis=-1, keepdims=True)
    return (scaled - mean_one - xh * mean_two) * rstd


def col_sum(value):
    return jnp.sum(value, axis=0, keepdims=True)


class Swap:
    def __init__(self, me, send, recv, ssem, rsem, chunks):
        self.me, self.send, self.recv, self.ssem, self.rsem = me, send, recv, ssem, rsem
        self.rows = send.shape[1] // chunks
        self.chunks = chunks
        self.turn = 0

    def copy(self, slot, i):
        rows = rows_of(i, self.rows)
        return remote(
            self.send.at[slot, rows],
            self.recv.at[slot, rows],
            self.ssem.at[slot, i],
            self.rsem.at[slot, i],
            self.me.core(),
        )

    def run(self, part, between, post):
        slot = self.turn % 2
        self.turn += 1

        @pl.loop(0, self.chunks)
        def _(i):
            rows = rows_of(i, self.rows)
            self.send[slot, rows] = part(rows).astype(BF)
            self.copy(slot, i).start()

        if between is not None:
            between()

        @pl.loop(0, self.chunks)
        def _(i):
            rows = rows_of(i, self.rows)
            self.copy(slot, i).wait()
            total = self.send[slot, rows].astype(F32) + self.recv[slot, rows].astype(F32)
            post(i, rows, total)


class Layer:
    def __init__(self, **kw):
        self.__dict__.update(kw)


def head_mask(layer, i, c):
    h = lax.rem(i, 3)
    half = jnp.where(h == 2, layer.third(c), lax.rem(h, 2))
    lane = lax.broadcasted_iota(jnp.int32, (1, 128), 1) // 64
    mask = jnp.where(lane == half, 1.0, 0.0).astype(BF)
    return i // 3, pl.ds(pl.multiple_of((h // 2) * 128, 128), 128), mask


def forward(layer, me, swap, bias_row, prm, done):
    L, c = layer, me.c
    units = L.q.shape[0]

    @pl.loop(0, units)
    def _(u):
        x = L.x[...]
        n = L.wq.shape[2]
        L.q[u, :, :n] = ((nn(x, L.wq[u]) + L.bias_q(u)).astype(BF) * 0.125).astype(BF)
        L.k[u, :, :n] = nn(x, L.wk[u]).astype(BF)
        L.v[u, :, :n] = (nn(x, L.wv[u]) + L.bias_v(u)).astype(BF)
        if n < 256:
            pad = jnp.zeros((x.shape[0], 256 - n), BF)
            L.q[u, :, n:] = pad
            L.k[u, :, n:] = pad
            L.v[u, :, n:] = pad
        L.o[u] = jnp.zeros(L.o.shape[1:], BF)

    @pl.loop(0, 3 * units)
    def _(i):
        u, cols, mask = head_mask(L, i, c)
        k = L.k[u, :, cols]
        v = L.v[u, :, cols] * mask
        for ch in range(4):
            rows = pl.ds(ch * 128, 128)
            scores = nt(L.q[u, rows, cols] * mask, k) + bias_row[0:1, :]
            top = jnp.max(scores, axis=-1, keepdims=True)
            expo = jnp.exp(scores - top)
            inv = 1.0 / jnp.sum(expo, axis=-1, keepdims=True)
            probs = (expo * inv).astype(BF)
            L.p[i, rows] = probs
            L.o[u, rows, cols] = L.o[u, rows, cols] + nn(probs, v).astype(BF)

    def attn_part(rows):
        n = L.wo.shape[1]
        total = nn(L.o[0, rows, :n], L.wo[0])
        for u in range(1, units):
            total = total + nn(L.o[u, rows, :n], L.wo[u])
        return total

    def attn_post(i, rows, total):
        value = L.x[rows].astype(F32) + total + prm[L.prow : L.prow + 1, :]
        xh, rstd = norm_parts(value)
        L.xh1[rows] = xh
        L.rs1[rows] = rstd
        L.a[rows] = (xh * prm[L.prow + 1 : L.prow + 2, :] + prm[L.prow + 2 : L.prow + 3, :]).astype(BF)

    swap.run(attn_part, None, attn_post)

    @pl.loop(0, 4)
    def _(j):
        pre = nn(L.a[...], L.wi[j]) + L.bias_i(j)
        sq = pre * pre
        t = jnp.tanh(0.7978845608028654 * pre * (1.0 + 0.044715 * sq))
        half = 0.5 * (1.0 + t)
        L.g[j] = (pre * half).astype(BF)
        slope = half + 0.5 * pre * (1.0 - t * t) * (0.7978845608028654 + 0.7978845608028654 * 0.134145 * sq)
        L.gp[j] = slope.astype(BF)

    def ffn_part(rows):
        total = nn(L.g[0, rows], L.wf[0])
        for j in range(1, 4):
            total = total + nn(L.g[j, rows], L.wf[j])
        return total

    def ffn_post(i, rows, total):
        value = L.a[rows].astype(F32) + total + prm[L.prow + 3 : L.prow + 4, :]
        xh, rstd = norm_parts(value)
        L.xh2[rows] = xh
        L.rs2[rows] = rstd
        done(rows, xh * prm[L.prow + 4 : L.prow + 5, :] + prm[L.prow + 5 : L.prow + 6, :])

    swap.run(ffn_part, None, ffn_post)


def backward(layer, me, swap, prm, sums, upstream, done):
    L, c = layer, me.c
    units = L.q.shape[0]
    prow = L.prow
    n_rows = L.x.shape[0]
    for i in range(6):
        sums[prow + i : prow + i + 1, :] = jnp.zeros((1, 768), F32)

    @pl.loop(0, n_rows // 128)
    def _(i):
        rows = rows_of(i, 128)
        dy = upstream(rows)
        xh = L.xh2[rows]
        sums[prow + 4 : prow + 5, :] += col_sum(dy * xh)
        sums[prow + 5 : prow + 6, :] += col_sum(dy)
        df = norm_grad(xh, L.rs2[rows], prm[prow + 4 : prow + 5, :], dy)
        low = df.astype(BF)
        sums[prow + 3 : prow + 4, :] += col_sum(low.astype(F32))
        L.df[rows] = df
        L.dr[rows] = low

    @pl.loop(0, 4)
    def _(j):
        dpre = (nt(L.dr[...], L.wf[j]) * L.gp[j].astype(F32)).astype(BF)
        L.gp[j] = dpre
        n = dpre.shape[1]
        sums[pl.ds(L.brow + j, 1), :n] = col_sum(dpre.astype(F32))

    def ffn_part(rows):
        total = nt(L.gp[0, rows], L.wi[0])
        for j in range(1, 4):
            total = total + nt(L.gp[j, rows], L.wi[j])
        return total

    def ffn_weights():
        @pl.loop(0, 4)
        def _(j):
            L.gwf[j] = tn(L.g[j], L.dr[...]).astype(BF)
            L.gwi[j] = tn(L.a[...], L.gp[j]).astype(BF)

    def ffn_post(i, rows, total):
        da = L.df[rows] + total
        xh = L.xh1[rows]
        sums[prow + 1 : prow + 2, :] += col_sum(da * xh)
        sums[prow + 2 : prow + 3, :] += col_sum(da)
        dh = norm_grad(xh, L.rs1[rows], prm[prow + 1 : prow + 2, :], da)
        low = dh.astype(BF)
        sums[prow : prow + 1, :] += col_sum(low.astype(F32))
        L.df[rows] = dh
        L.dr[rows] = low

    swap.run(ffn_part, ffn_weights, ffn_post)

    @pl.loop(0, units)
    def _(u):
        n = L.wo.shape[1]
        L.do[u, :, :n] = nt(L.dr[...], L.wo[u]).astype(BF)
        if n < 256:
            L.do[u, :, n:] = jnp.zeros((n_rows, 256 - n), BF)
        for ref in (L.dq, L.dk, L.dv):
            ref[u] = jnp.zeros(ref.shape[1:], BF)

    @pl.loop(0, 3 * units)
    def _(i):
        u, cols, mask = head_mask(L, i, c)
        k = L.k[u, :, cols] * mask
        v = L.v[u, :, cols]
        for ch in range(4):
            rows = pl.ds(ch * 128, 128)
            d_probs = nt(L.do[u, rows, cols] * mask, v)
            probs = L.p[i, rows].astype(F32)
            both = probs * d_probs
            d_scores = (both - probs * jnp.sum(both, axis=-1, keepdims=True)).astype(BF)
            L.ds[rows] = d_scores
            L.dq[u, rows, cols] = L.dq[u, rows, cols] + (nn(d_scores, k) * 0.125).astype(BF)
        L.dv[u, :, cols] = L.dv[u, :, cols] + tn(L.p[i], L.do[u, :, cols] * mask).astype(BF)
        L.dk[u, :, cols] = L.dk[u, :, cols] + tn(L.ds[...], L.q[u, :, cols] * mask).astype(BF)

    def attn_part(rows):
        n = L.wq.shape[2]
        total = None
        for u in range(units):
            for grad, weight in ((L.dq, L.wq), (L.dk, L.wk), (L.dv, L.wv)):
                term = nt(grad[u, rows, :n], weight[u])
                total = term if total is None else total + term
        return total

    def attn_weights():
        @pl.loop(0, units)
        def _(u):
            n = L.gwo.shape[1]
            L.gwo[u] = tn(L.o[u, :, :n], L.dr[...]).astype(BF)
            x = L.x[...]
            for grad, out in ((L.dq, L.gwq), (L.dk, L.gwk), (L.dv, L.gwv)):
                out[u] = tn(x, grad[u, :, :n]).astype(BF)
            sums[pl.ds(L.qrow + u, 1), :256] = col_sum(L.dq[u].astype(F32))
            sums[pl.ds(L.qrow + units + u, 1), :256] = col_sum(L.dv[u].astype(F32))

    def attn_post(i, rows, total):
        done(rows, L.df[rows] + total)

    swap.run(attn_part, attn_weights, attn_post)


def compute_kernel(*refs):
    me = Place()
    c = me.c
    (X, CT, LN, PRM, BP, WQ, WK, WV, WO, WI, WF, SQ, SK, SV, SO, SI, SF) = refs[:17]
    (Y, DX, SM, GQ, GK, GV, GO, GI, GF, GSQ, GSK, GSV, GSO, GSI, GSF) = refs[17:32]
    (
        bias_row, send, recv, ssem, rsem,
        q, k, v, o, p, xh1, rs1, a, g, gp, xh2, rs2, df, dr, do, dq, dk, dv, ds,
        wsq, wsk, wsv, wso, x2, q2, k2, v2, o2, p2, xh12, rs12, a2, g2, gp2, xh22, rs22, dx2,
    ) = refs[32:]

    barrier = pltpu.get_barrier_semaphore()
    pl.semaphore_signal(barrier, inc=1, device_id=me.core(), device_id_type=MESH)
    pl.semaphore_wait(barrier, 1)

    n_keys = X.shape[0]
    position = lax.broadcasted_iota(jnp.int32, (8, n_keys), 1).astype(F32)
    bias_row[...] = jnp.where(position < LN[0:8, 0:1], 0.0, MASKED)
    SM[...] = jnp.zeros(SM.shape, F32)
    first = pl.ds(pl.multiple_of(c * 256, 128), 128)
    for src, dst in ((SQ, wsq), (SK, wsk), (SV, wsv)):
        dst[0, :, 0:128] = src[:, first]
        dst[0, :, 128:256] = src[:, 128:256]
    wso[0, 0:128, :] = SO[first, :]
    wso[0, 128:256, :] = SO[128:256, :]
    s_bias = pl.ds(pl.multiple_of(c * 256, 128), 128)
    v_bias = pl.ds(pl.multiple_of(384 + c * 256, 128), 128)

    teacher = Layer(
        x=X, wq=WQ, wk=WK, wv=WV, wo=WO, wi=WI, wf=WF, q=q, k=k, v=v, o=o, p=p, xh1=xh1, rs1=rs1, a=a, g=g, gp=gp,
        xh2=xh2, rs2=rs2, df=df, dr=dr, do=do, dq=dq, dk=dk, dv=dv, ds=ds, prow=0, qrow=12, brow=16,
        gwq=GQ, gwk=GK, gwv=GV, gwo=GO, gwi=GI, gwf=GF,
        bias_q=lambda u: BP[2 * c + u, 0:1, 0:192],
        bias_v=lambda u: BP[2 * c + u, 3:4, 0:192],
        bias_i=lambda j: BP[j, 1:2, :],
        third=lambda c: 0,
    )
    student = Layer(
        x=x2, wq=wsq, wk=wsk, wv=wsv, wo=wso, wi=SI, wf=SF, q=q2, k=k2, v=v2, o=o2, p=p2, xh1=xh12, rs1=rs12, a=a2,
        g=g2, gp=gp2, xh2=xh22, rs2=rs22, df=df, dr=dr, do=do, dq=dq, dk=dk, dv=dv, ds=ds, prow=6, qrow=24, brow=20,
        gwq=GSQ, gwk=GSK, gwv=GSV, gwo=GSO, gwi=GSI, gwf=GSF,
        bias_q=lambda u: jnp.concatenate([PRM[12:13, s_bias], PRM[12:13, 128:256]], axis=1),
        bias_v=lambda u: jnp.concatenate([PRM[12:13, v_bias], PRM[12:13, 512:640]], axis=1),
        bias_i=lambda j: BP[j, 2:3, 0 : SI.shape[2]],
        third=lambda c: c,
    )
    swap = Swap(me, send, recv, ssem, rsem, 4)

    def to_student(rows, value):
        x2[rows] = value.astype(BF)

    def to_output(rows, value):
        Y[rows] = value.astype(BF)

    def between(rows, value):
        dx2[rows] = value

    def to_grad(rows, value):
        DX[rows] = value.astype(BF)

    forward(teacher, me, swap, bias_row, PRM, to_student)
    forward(student, me, swap, bias_row, PRM, to_output)
    backward(student, me, swap, PRM, SM, lambda rows: CT[rows].astype(F32), between)
    backward(teacher, me, swap, PRM, SM, lambda rows: dx2[rows], to_grad)


def add_up(refs):
    total = refs[0][...].astype(F32)
    for ref in refs[1:]:
        total = total + ref[...].astype(F32)
    return total


def reduce_kernel(*refs):
    me = Place()
    r, z, s, c = me.r, me.z, me.s, me.c
    names = 12
    Y, DX, SM = refs[:3]
    grads = refs[3 : 3 + names]
    YO, DO, SUMS = refs[3 + names : 6 + names]
    outs = refs[6 + names : 6 + 2 * names]
    rest = refs[6 + 2 * names :]
    R1, S1, R2, S2 = rest[:names], rest[names : 2 * names], rest[2 * names : 3 * names], rest[3 * names : 4 * names]
    (s1s, s1r, s2s, s2r, s3s, s3r, cs, cr, ys, yr, sml, sms, smr, zs3, zr3) = rest[4 * names :]
    greet(me)
    owner = z // 2 == c

    def kind(w):
        return 0 if w < 4 else (1 if w < 8 else 2)

    for w in range(names):
        quarter = grads[w].shape[1] // 4
        for k in (1, 2, 3):
            part = grads[w].at[:, rows_of(me.plane_index(k), quarter)]
            remote(part, R1[w].at[k - 1], s1s.at[w, k - 1], s1r.at[w, k - 1], me.plane(k)).start()

    @pl.when(owner)
    def _():
        for a, (src, dst) in enumerate(((Y, YO), (DX, DO))):
            pltpu.make_async_copy(src.at[rows_of(z, 128)], dst.at[z % 2], yr.at[a, z % 2]).start()
            for d in (1, 2, 3):
                remote(
                    src.at[rows_of(me.line_index(d), 128)], dst.at[z % 2], ys.at[a, d - 1], yr.at[a, z % 2], me.line(d)
                ).start()

    sml[0] = SM[...]
    for d in (1, 2, 3):
        remote(sml.at[0], sml.at[d], sms.at[d - 1], smr.at[d - 1], me.line(d)).start()
    for d in (1, 2, 3):
        remote(sml.at[0], sml.at[d], sms.at[d - 1], smr.at[d - 1], me.line(d)).wait()
    sml[4] = add_up([sml.at[i] for i in range(4)])
    for k in (1, 2, 3):
        remote(sml.at[4], sml.at[4 + k], sms.at[2 + k], smr.at[2 + k], me.plane(k)).start()
    for k in (1, 2, 3):
        remote(sml.at[4], sml.at[4 + k], sms.at[2 + k], smr.at[2 + k], me.plane(k)).wait()
    SUMS[0] = add_up([sml.at[4 + i] for i in range(4)])
    other_sums = remote(SUMS.at[0], SUMS.at[1], sms.at[6], smr.at[6], me.core())
    other_sums.start()

    for w in range(names):
        quarter = grads[w].shape[1] // 4
        own = grads[w].at[:, rows_of(r, quarter)]
        for k in (1, 2, 3):
            remote(own, R1[w].at[k - 1], s1s.at[w, k - 1], s1r.at[w, k - 1], me.plane(k)).wait()
        S1[w][...] = add_up([own] + [R1[w].at[k] for k in range(3)]).astype(BF)
        if kind(w) == 0:
            for u in range(2):
                target = 2 * c + u

                @pl.when(target != z)
                def _():
                    slot = lax.rem(target - z + 4, 4) - 1
                    remote(S1[w].at[u], R2[w].at[slot], s2s.at[w, u], s2r.at[w, slot], (r, target, s)).start()

        elif kind(w) == 1:
            for d in (1, 2, 3):
                remote(
                    S1[w].at[me.line_index(d)], R2[w].at[d - 1], s2s.at[w, d - 1], s2r.at[w, d - 1], me.line(d)
                ).start()
        else:
            sub = quarter // 4
            for d in (1, 2, 3):
                remote(
                    S1[w].at[0, rows_of(me.line_index(d), sub)],
                    R2[w].at[d - 1],
                    s2s.at[w, d - 1],
                    s2r.at[w, d - 1],
                    me.line(d),
                ).start()

    for w in range(names):
        quarter = grads[w].shape[1] // 4
        if kind(w) == 0:
            for u in range(2):

                @pl.when(2 * c + u != z)
                def _():
                    remote(S1[w].at[u], R2[w].at[0], s2s.at[w, u], s2r.at[w, 0], me.core()).wait_send()

            @pl.when(owner)
            def _():
                for d in (1, 2, 3):
                    remote(S1[w].at[0], R2[w].at[d - 1], s2s.at[w, 0], s2r.at[w, d - 1], me.core()).wait_recv()
                mine = rows_of(r, quarter)
                outs[w][mine] = add_up([S1[w].at[z % 2]] + [R2[w].at[d] for d in range(3)]).astype(BF)
                for k in (1, 2, 3):
                    remote(
                        outs[w].at[mine], outs[w].at[mine], s3s.at[w, k - 1], s3r.at[w, k - 1], me.plane(k)
                    ).start()

        elif kind(w) == 1:
            for d in (1, 2, 3):
                remote(S1[w].at[0], R2[w].at[d - 1], s2s.at[w, d - 1], s2r.at[w, d - 1], me.line(d)).wait()
            mine = rows_of(r, quarter)
            outs[w][mine] = add_up([S1[w].at[z]] + [R2[w].at[d] for d in range(3)]).astype(BF)
            for k in (1, 2, 3):
                remote(outs[w].at[mine], outs[w].at[mine], s3s.at[w, k - 1], s3r.at[w, k - 1], me.plane(k)).start()
        else:
            sub = quarter // 4
            for d in (1, 2, 3):
                remote(
                    S1[w].at[0, rows_of(0, sub)], R2[w].at[d - 1], s2s.at[w, d - 1], s2r.at[w, d - 1], me.line(d)
                ).wait()
            mine = rows_of(r * 4 + z, sub)
            outs[w][0, mine] = add_up([S1[w].at[0, rows_of(z, sub)]] + [R2[w].at[d] for d in range(3)]).astype(BF)
            for d in (1, 2, 3):
                remote(
                    outs[w].at[0, mine], outs[w].at[0, mine], zs3.at[w - 8, d - 1], zr3.at[w - 8, d - 1], me.line(d)
                ).start()

    for w in range(8, names):
        quarter = grads[w].shape[1] // 4
        sub = quarter // 4
        for d in (1, 2, 3):
            theirs = rows_of(r * 4 + me.line_index(-d), sub)
            remote(
                outs[w].at[0, theirs], outs[w].at[0, theirs], zs3.at[w - 8, d - 1], zr3.at[w - 8, d - 1], me.line(d)
            ).wait()
        mine = rows_of(r, quarter)
        for k in (1, 2, 3):
            remote(
                outs[w].at[0, mine], outs[w].at[0, mine], s3s.at[w, k - 1], s3r.at[w, k - 1], me.plane(k)
            ).start()

    for w in range(names):
        quarter = grads[w].shape[1] // 4

        def gathered(ref):
            for k in (1, 2, 3):
                theirs = rows_of(me.plane_index(k), quarter)
                remote(ref.at[theirs], ref.at[theirs], s3s.at[w, k - 1], s3r.at[w, k - 1], me.plane(k)).wait()

        if kind(w) == 0:

            @pl.when(owner)
            def _():
                gathered(outs[w])
                remote(outs[w], outs[w], cs.at[w], cr.at[w], me.core()).start()

        elif kind(w) == 1:
            gathered(outs[w])
        else:
            gathered(outs[w].at[0])
            remote(outs[w].at[0], outs[w].at[1], cs.at[w], cr.at[w], me.core()).start()
    for w in range(names):
        if kind(w) == 0:

            @pl.when(owner)
            def _():
                remote(outs[w], outs[w], cs.at[w], cr.at[w], me.core()).wait_send()

            @pl.when(jnp.logical_not(owner))
            def _():
                remote(outs[w], outs[w], cs.at[w], cr.at[w], me.core()).wait_recv()

        elif kind(w) == 2:
            remote(outs[w].at[0], outs[w].at[1], cs.at[w], cr.at[w], me.core()).wait()
    other_sums.wait()

    @pl.when(owner)
    def _():
        for a, (src, dst) in enumerate(((Y, YO), (DX, DO))):
            for d in (1, 2, 3):
                remote(src.at[rows_of(0, 128)], dst.at[0], ys.at[a, d - 1], yr.at[a, 0], me.core()).wait_send()

    for a, (src, dst) in enumerate(((Y, YO), (DX, DO))):
        for j in range(2):
            chip = 2 * c + j

            @pl.when(chip == z)
            def _():
                pltpu.make_async_copy(src.at[rows_of(0, 128)], dst.at[j], yr.at[a, j]).wait()

            @pl.when(chip != z)
            def _():
                remote(src.at[rows_of(0, 128)], dst.at[j], ys.at[a, 0], yr.at[a, j], me.core()).wait_recv()


def final_kernel(*refs):
    z = lax.axis_index("head")
    c = lax.rem(lax.axis_index("seq"), 2)
    YO, DO, SUMS = refs[:3]
    grads = refs[3:15]
    outs = refs[15:]
    outs[0][...] = YO[...].astype(F32)
    outs[1][...] = DO[...].astype(F32)

    def whole(at, w):
        outs[at][...] = grads[w][...].astype(F32)

    whole(2, 0)
    whole(4, 1)
    whole(5, 2)
    whole(7, 3)
    whole(11, 4)
    whole(13, 5)
    whole(26, 6)
    whole(28, 7)
    near = pl.ds(pl.multiple_of(c * 256, 128), 128)
    far = pl.ds(pl.multiple_of((1 - c) * 256, 128), 128)
    for at, w in ((17, 8), (19, 9), (20, 10)):
        g = grads[w]
        outs[at][:, near] = g[0, :, 0:128].astype(F32)
        outs[at][:, far] = g[1, :, 0:128].astype(F32)
        outs[at][:, 128:256] = g[0, :, 128:256].astype(F32) + g[1, :, 128:256].astype(F32)
    g = grads[11]
    outs[22][near, :] = g[0, 0:128, :].astype(F32)
    outs[22][far, :] = g[1, 0:128, :].astype(F32)
    outs[22][128:256, :] = g[0, 128:256, :].astype(F32) + g[1, 128:256, :].astype(F32)

    for i, at in enumerate((8, 9, 10, 14, 15, 16, 23, 24, 25, 29, 30, 31)):
        outs[at][...] = SUMS[0, i : i + 1, :]
    side = jnp.where(z // 2 == c, 0, 1)
    outs[3][...] = SUMS[side, pl.ds(12 + z % 2, 1), 0:192]
    outs[6][...] = SUMS[side, pl.ds(14 + z % 2, 1), 0:192]
    outs[12][...] = SUMS[0, pl.ds(16 + z, 1), 0 : outs[12].shape[1]]
    outs[27][...] = SUMS[0, pl.ds(20 + z, 1), 0 : outs[27].shape[1]]
    for at, row in ((18, 24), (21, 25)):
        outs[at][:, near] = SUMS[0, row : row + 1, 0:128]
        outs[at][:, far] = SUMS[1, row : row + 1, 0:128]
        outs[at][:, 128:256] = SUMS[0, row : row + 1, 128:256] + SUMS[1, row : row + 1, 128:256]


ANYWHERE = pl.BlockSpec(memory_space=pl.ANY)
IN_VMEM = pl.BlockSpec(memory_space=pltpu.VMEM)


def shape(*dims, kind=BF):
    return jax.ShapeDtypeStruct(dims, kind)


def body(
    tokens, lengths, cotangent,
    t_query, t_query_bias, t_key, t_value, t_value_bias, t_attn_out, t_attn_bias, t_norm1_gain, t_norm1_bias,
    t_ffn_in, t_ffn_in_bias, t_ffn_out, t_ffn_out_bias, t_norm2_gain, t_norm2_bias,
    s_query, s_query_bias, s_key, s_value, s_value_bias, s_attn_out, s_attn_bias, s_norm1_gain, s_norm1_bias,
    s_ffn_in, s_ffn_in_bias, s_ffn_out, s_ffn_out_bias, s_norm2_gain, s_norm2_bias,
):
    seq_size = lax.axis_size("seq")
    outer = seq_size // 2
    groups = [[2 * y + core for y in range(outer)] for core in range(2)]

    def widen(value, axis):
        if outer == 1:
            return value
        return lax.all_gather(value, "seq", axis=axis, tiled=True, axis_index_groups=groups)

    t_ffn_in, t_ffn_in_bias, t_ffn_out = widen(t_ffn_in, 1), widen(t_ffn_in_bias, 0), widen(t_ffn_out, 0)
    s_ffn_in, s_ffn_in_bias, s_ffn_out = widen(s_ffn_in, 1), widen(s_ffn_in_bias, 0), widen(s_ffn_out, 0)

    def wide(value, width):
        return jnp.pad(value.astype(F32), (0, width - value.shape[0]))

    n_in, n_s = t_ffn_in.shape[1], s_ffn_in.shape[1]
    pack = jnp.stack([wide(v, n_in) for v in (t_query_bias, t_ffn_in_bias, s_ffn_in_bias, t_value_bias)])
    pack = jnp.pad(pack, ((0, 4), (0, 0)))
    lens = jnp.broadcast_to(lengths.astype(F32)[:, None, None], (2, 8, 128))
    params = jnp.stack(
        [
            t_attn_bias, t_norm1_gain, t_norm1_bias, t_ffn_out_bias, t_norm2_gain, t_norm2_bias,
            s_attn_bias, s_norm1_gain, s_norm1_bias, s_ffn_out_bias, s_norm2_gain, s_norm2_bias,
            jnp.concatenate([s_query_bias, s_value_bias]),
        ]
    )
    params = jnp.pad(params, ((0, 3), (0, 0)))

    dma = pltpu.SemaphoreType.DMA
    gathered = pl.pallas_call(
        gather_kernel,
        out_shape=[
            shape(4, 128, 768), shape(4, 128, 768), shape(8, 128, kind=F32), shape(4, 8, n_in, kind=F32),
            shape(2, 768, 192), shape(2, 768, 192), shape(2, 768, 192), shape(2, 192, 768),
            shape(4, 768, n_in), shape(4, n_in, 768), shape(4, 768, n_s), shape(4, n_s, 768),
        ],
        in_specs=[ANYWHERE] * 12,
        out_specs=[ANYWHERE] * 12,
        scratch_shapes=[
            dma((9, 3)), dma((9, 3)), dma((8, 3, 3)), dma((8, 3, 3)), dma((10,)), dma((2, 2)), dma((2, 4)), dma((3, 4)), dma((3, 4)),
        ],
        compiler_params=pltpu.CompilerParams(collective_id=0, has_side_effects=True),
        name="gather",
    )(tokens, cotangent, lens, pack, t_query, t_key, t_value, t_attn_out, t_ffn_in, t_ffn_out, s_ffn_in, s_ffn_out)
    (X, CT, LN, BP, WQ, WK, WV, WO, WI, WF, SI, SF) = gathered

    n = 512
    act = lambda *dims, kind=BF: pltpu.VMEM(dims, kind)
    results = pl.pallas_call(
        compute_kernel,
        out_shape=[
            shape(n, 768), shape(n, 768), shape(32, 768, kind=F32),
            shape(2, 768, 192), shape(2, 768, 192), shape(2, 768, 192), shape(2, 192, 768),
            shape(4, 768, n_in), shape(4, n_in, 768),
            shape(1, 768, 256), shape(1, 768, 256), shape(1, 768, 256), shape(1, 256, 768),
            shape(4, 768, n_s), shape(4, n_s, 768),
        ],
        in_specs=[IN_VMEM] * 17,
        out_specs=[IN_VMEM] * 15,
        scratch_shapes=[
            act(8, n, kind=F32), act(2, n, 768), act(2, n, 768), dma((2, 4)), dma((2, 4)),
            act(2, n, 256), act(2, n, 256), act(2, n, 256), act(2, n, 256), act(6, n, n),
            act(n, 768, kind=F32), act(n, 1, kind=F32), act(n, 768), act(4, n, n_in), act(4, n, n_in),
            act(n, 768, kind=F32), act(n, 1, kind=F32), act(n, 768, kind=F32), act(n, 768),
            act(2, n, 256), act(2, n, 256), act(2, n, 256), act(2, n, 256), act(n, n),
            act(1, 768, 256), act(1, 768, 256), act(1, 768, 256), act(1, 256, 768),
            act(n, 768), act(1, n, 256), act(1, n, 256), act(1, n, 256), act(1, n, 256), act(3, n, n),
            act(n, 768, kind=F32), act(n, 1, kind=F32), act(n, 768), act(4, n, n_s), act(4, n, n_s),
            act(n, 768, kind=F32), act(n, 1, kind=F32), act(n, 768, kind=F32),
        ],
        compiler_params=pltpu.CompilerParams(collective_id=1, has_side_effects=True, vmem_limit_bytes=VMEM_LIMIT),
        name="compute",
    )(
        X.reshape(n, 768), CT.reshape(n, 768), LN, params, BP, WQ, WK, WV, WO, WI, WF,
        s_query, s_key, s_value, s_attn_out, SI, SF,
    )
    (Y, DX, SM, GQ, GK, GV, GO, GI, GF, GSQ, GSK, GSV, GSO, GSI, GSF) = results

    grads = (GQ, GK, GV, GO, GI, GF, GSI, GSF, GSQ, GSK, GSV, GSO)
    names = len(grads)

    def one(g):
        count, rows, cols = g.shape
        return rows // 4, cols, count

    r1 = [pltpu.VMEM((3, one(g)[2], one(g)[0], one(g)[1]), BF) for g in grads]
    s1 = [pltpu.VMEM((one(g)[2], one(g)[0], one(g)[1]), BF) for g in grads]
    pieces = [(one(g)[0] if w < 8 else one(g)[0] // 4, one(g)[1]) for w, g in enumerate(grads)]
    r2 = [pltpu.VMEM((3,) + p, BF) for p in pieces]
    s2 = [pltpu.VMEM(p if w < 0 else (16, 128), BF) for w, p in enumerate(pieces)]
    reduced = pl.pallas_call(
        reduce_kernel,
        out_shape=[shape(2, 128, 768), shape(2, 128, 768), shape(2, 32, 768, kind=F32)]
        + [shape(*g.shape[1:]) if w < 8 else shape(2, *g.shape[1:]) for w, g in enumerate(grads)],
        in_specs=[IN_VMEM] * (3 + names),
        out_specs=[IN_VMEM] * (3 + names),
        scratch_shapes=r1 + s1 + r2 + s2
        + [
            dma((names, 3)), dma((names, 3)), dma((names, 3)), dma((names, 3)), dma((names, 3)), dma((names, 3)),
            dma((names,)), dma((names,)), dma((2, 3)), dma((2, 2)),
            pltpu.VMEM((8, 32, 768), F32), dma((7,)), dma((7,)), dma((4, 3)), dma((4, 3)),
        ],
        compiler_params=pltpu.CompilerParams(collective_id=2, has_side_effects=True, vmem_limit_bytes=VMEM_LIMIT),
        name="reduce",
    )(Y, DX, SM, *grads)
    reduced = list(reduced)

    if outer > 1:
        reduced[2] = lax.psum(reduced[2].reshape(2, 32, 768), "seq", axis_index_groups=groups)
        reduced[3:] = [
            lax.psum(g.astype(F32), "seq", axis_index_groups=groups).astype(BF) for g in reduced[3:]
        ]

    f = functools.partial(shape, kind=F32)
    final_shapes = [
        f(2, 128, 768), f(2, 128, 768),
        f(768, 192), f(1, 192), f(768, 192), f(768, 192), f(1, 192), f(192, 768),
        f(1, 768), f(1, 768), f(1, 768), f(768, n_in), f(1, n_in), f(n_in, 768), f(1, 768), f(1, 768), f(1, 768),
        f(768, 384), f(1, 384), f(768, 384), f(768, 384), f(1, 384), f(384, 768),
        f(1, 768), f(1, 768), f(1, 768), f(768, n_s), f(1, n_s), f(n_s, 768), f(1, 768), f(1, 768), f(1, 768),
    ]
    outs = list(
        pl.pallas_call(
            final_kernel,
            out_shape=final_shapes,
            in_specs=[IN_VMEM] * (3 + names),
            out_specs=[IN_VMEM] * len(final_shapes),
            compiler_params=pltpu.CompilerParams(vmem_limit_bytes=VMEM_LIMIT),
            name="final",
        )(*reduced)
    )
    for i, o in enumerate(outs):
        if o.shape[0] == 1:
            outs[i] = o.reshape(-1)
    if outer > 1:
        y = lax.axis_index("seq") // 2
        for i, axis in ((11, 1), (12, 0), (13, 0), (26, 1), (27, 0), (28, 0)):
            width = outs[i].shape[axis] // outer
            outs[i] = lax.dynamic_slice_in_dim(outs[i], y * width, width, axis)
    return tuple(outs)


def solution(mesh):
    seqs = P(("row", "seq"), "head", None)
    col, line, row = P(None, "head"), P("head"), P("head", None)
    fcol, fline, frow = P(None, ("head", "seq")), P(("head", "seq")), P(("head", "seq"), None)
    rep = P()
    teacher = (col, line, col, col, line, row, rep, rep, rep, fcol, fline, frow, rep, rep, rep)
    student = (rep,) * 9 + (fcol, fline, frow, rep, rep, rep)
    return jax.shard_map(
        body,
        mesh=mesh,
        in_specs=(seqs, P(("row", "seq")), seqs) + teacher + student,
        out_specs=(seqs, seqs) + teacher + student,
        check_vma=False,
    )
```

time: 1320 us -> 550 us (0.42)
  waiting for transfers between devices: 1010 us -> 0 us
  Pallas kernels: 0 us -> 500 us
  matrix products: 122 us -> 0 us
  blocking collectives: 64 us -> 0 us
  local copies, waits for them, and re-layouts: 47.7 us -> 21.9 us
  other arithmetic: 44.1 us -> 22 us
  between operations: 15.8 us -> 0.76 us
    pallas_call x0 -> x4, Pallas kernels: none -> 500 us  [the longest x1 237 us: body(): pl.pallas_call(reduce_kernel, out_shape=[shape(2, 128, 768), shape(2, 128...]
    reduce_scatter x8 -> x0, waiting for transfers between devices: 452 us -> none  [the longest x2 138 us: ffn_by_tokens(): lax.psum_scatter(jnp.dot(hidden, w_back, preferred_element_type=jnp.float...]
    all_gather x8 -> x0, waiting for transfers between devices: 298 us -> none  [the longest x2 76.8 us: ffn_by_tokens(): gathered = lax.all_gather(rows_low, ('head', 'seq'), axis=0, tiled=True)]
    psum x3 -> x0, waiting for transfers between devices: 263 us -> none  [the longest x1 98.4 us: body(): lax.psum((ffn_grads_t[0], ffn_grads_t[1], ffn_grads_t[2], ffn_grads_s[0],...]
    dot_general x48 -> x0, matrix products: 122 us -> none  [the longest x2 12.5 us: ffn_back_tokens(): jnp.einsum('rd,nd->rn', grads_all, w_back, preferred_element_type=jnp.flo...]
    psum x3 -> x0, blocking collectives: 64 us -> none  [the longest x1 40.4 us: body(): lax.psum((attn_grads_s[0], attn_grads_s[1], attn_grads_s[2], attn_grads_s...]
    reduce_sum x26 -> x0, other arithmetic: 32.2 us -> none  [the longest x8 11.8 us: layer_norm(): return center * lax.rsqrt(spread + EPSILON) * gain + shift]
    pallas_call x0 -> x15, other arithmetic: none -> 19.3 us  [body(): pl.pallas_call(final_kernel, out_shape=final_shapes, in_specs=[IN_VMEM] *...]
  transfers between devices with their start and end apart: 19 -> 0, of which waited for: 18 -> 0; matrix products, arithmetic and copies ran while one was open for 4% -> 0% of each run, Pallas kernels for 0% -> 0%
where the time goes in v1:
time: 550 us; the launch traced here: 545 us
  Pallas kernels  500 us (91%)
  other arithmetic  22 us (4%)
  local copies, waits for them, and re-layouts  21.9 us (4%)
    pallas_call x1, Pallas kernels, body(): pl.pallas_call(reduce_kernel, out_shape=[shape(2, 128, 768), shape(2, 128...  237 us
    pallas_call x1, Pallas kernels, body(): pl.pallas_call(gather_kernel, out_shape=[shape(4, 128, 768), shape(4, 128...  165 us
    pallas_call x1, Pallas kernels, body(): pl.pallas_call(compute_kernel, out_shape=[shape(n, 768), shape(n, 768), s...  89.8 us
    pallas_call x15, other arithmetic, body(): pl.pallas_call(final_kernel, out_shape=final_shapes, in_specs=[IN_VMEM] *...  19.3 us

profile of v1, /device:TPU:0, one launch (start us, length us, event | category | flops | bytes accessed | tf_op | source)
XLA Modules:
  0.0 544.7 jit_solution(4136350675312972902)
XLA Ops:
  0.7 0.7 convert_element_type.13
  1.4 0.7 reshape.145
  2.1 0.7 pad.19
  2.8 0.7 pad.21
  3.5 0.7 pad_convert_fusion
  4.1 0.7 stack.70
  4.8 0.7 stack.71
  5.5 0.7 stack.72
  6.2 0.7 stack.73
  6.9 0.7 stack.74
  7.6 0.7 stack.75
  8.3 0.7 stack.76
  9.0 0.7 stack.77
  9.7 0.7 stack.78
  10.4 0.7 stack.79
  11.1 0.7 stack.80
  11.8 0.7 stack.81
  12.5 0.7 pad_maximum_fusion
  13.2 0.6 select_maximum_fusion.refs_3_
  13.8 0.7 broadcast_in_dim.2.refs_2_
  14.5 0.6 pad.23.refs_3_
  15.2 1.9 copy.65.refs_4_
  17.0 0.9 copy.66.refs_5_
  18.0 0.9 copy.67.refs_6_
  18.9 0.9 copy.68.refs_10_
  19.8 164.8 %gather.1 = (bf16[4,128,768]{2,1,0:T(8,128)(2,1)}, bf16[4,128,768]{2,1,0:T(8,128)(2,1)}, f32[8,128]{1,0:T(8,128)}, f32[4,8,384]{2,1,0:T(8,128)}, bf16[2,768,192]...) custom-call(bf16[2,128,768]{2,1,0:T(8,128)(2,1)} %refs_0_.1, ...), custom_call_target="tpu_custom_call" | custom-call | tf_op jit(solution)/shard_map/gather/pallas_call | solution.py:784
  184.6 89.8 %compute.1 = (bf16[512,768]{1,0:T(8,128)(2,1)}, bf16[512,768]{1,0:T(8,128)(2,1)}, f32[32,768]{1,0:T(8,128)}, bf16[2,768,192]{2,1,0:T(8,128)(2,1)}, bf16[2,768,19...) custom-call(bf16[512,768]{1,0:T(8,128)(2,1)} %bitcast.5, ...), custom_call_target="tpu_custom_call" | custom-call | tf_op jit(solution)/shard_map/compute/pallas_call | solution.py:803
  274.3 237.0 %reduce.16 = (bf16[2,128,768]{2,1,0:T(8,128)(2,1)}, bf16[2,128,768]{2,1,0:T(8,128)(2,1)}, f32[2,32,768]{2,1,0:T(8,128)}, bf16[768,192]{1,0:T(8,128)(2,1)}, bf16[...) custom-call(bf16[512,768]{1,0:T(8,128)(2,1)} %get-tuple-element.118., ...), custom_call_target="tpu_custom_call" | custom-call | tf_op jit(solution)/shard_map/reduce/pallas_call | solution.py:845
  511.4 8.5 %final.1 = (f32[2,128,768]{2,1,0:T(8,128)}, f32[2,128,768]{2,1,0:T(8,128)}, f32[768,192]{1,0:T(8,128)}, f32[1,192]{1,0:T(1,128)}, f32[768,192]{1,0:T(8,128)}, /*...) custom-call(bf16[2,128,768]{2,1,0:T(8,128)(2,1)} %get-tuple-element., ...), custom_call_target="tpu_custom_call" | custom-call | tf_op jit(solution)/shard_map/final/pallas_call | solution.py:877
  519.9 1.3 reduce.4
  521.3 1.3 reduce.8
  522.5 1.3 reduce.9
  523.8 1.3 reduce.1
  525.1 1.3 reduce.2
  526.4 1.3 reduce.3
  527.7 1.3 reduce.5
  529.0 1.3 reduce.6
  530.2 1.3 reduce.7
  531.5 1.3 reduce.10
  532.8 1.3 reduce.11
  534.1 1.3 reduce.12
  535.4 1.3 reduce.13
  536.7 1.3 reduce.14
  538.0 1.3 reduce.15
  539.2 2.3 copy.69
  541.5 1.1 copy.70
  542.6 1.1 copy.71
  543.7 1.1 copy.72
  (17 shorter events, 0.1 us)
Async XLA Ops:
  0.7 17.3 %copy-start.4 = (bf16[768,192]{0,1:T(8,128)(2,1)S(1)}, bf16[768,192]{0,1:T(8,128)(2,1)}, u32[]{:S(2)}) copy-start(bf16[768,192]{0,1:T(8,128)(2,1)} %param.39) | copy-start | bytes 884740
  0.7 16.4 %copy-start.3 = (bf16[768,192]{0,1:T(8,128)(2,1)S(1)}, bf16[768,192]{0,1:T(8,128)(2,1)}, u32[]{:S(2)}) copy-start(bf16[768,192]{0,1:T(8,128)(2,1)} %param.38) | copy-start | bytes 884740
  6.2 12.7 %copy-start.5 = (bf16[768,192]{0,1:T(8,128)(2,1)S(1)}, bf16[768,192]{0,1:T(8,128)(2,1)}, u32[]{:S(2)}) copy-start(bf16[768,192]{0,1:T(8,128)(2,1)} %param.60) | copy-start | bytes 884740
  519.9 21.6 %copy-start.2 = (f32[768,192]{1,0:T(8,128)S(1)}, f32[768,192]{1,0:T(8,128)}, u32[]{:S(2)}) copy-start(f32[768,192]{1,0:T(8,128)} %get-tuple-element.184) | copy-start | bytes 1769476
  539.2 3.3 copy-start.1
  541.5 2.1 copy-start

commit v2 on v1

v2 whole, which is shorter than its diff:
```python
import functools

import jax
import jax.numpy as jnp
from jax import lax
from jax.experimental import pallas as pl
from jax.experimental.pallas import tpu as pltpu
from jax.sharding import PartitionSpec as P

MESH = pl.DeviceIdType.MESH
F32 = jnp.float32
BF = jnp.bfloat16
EPS = 1e-5
MASKED = -1000000000.0
VMEM_LIMIT = 63 << 20


class Place:
    def __init__(self):
        self.r = lax.axis_index("row")
        self.z = lax.axis_index("head")
        self.s = lax.axis_index("seq")
        self.c = lax.rem(self.s, 2)

    def core(self):
        return (self.r, self.z, self.s + 1 - 2 * self.c)

    def line_index(self, step):
        return lax.rem(self.z + step + 4, 4)

    def line(self, step):
        return (self.r, self.line_index(step), self.s)

    def plane_index(self, k):
        if k == 1:
            return self.r + 1 - 2 * lax.rem(self.r, 2)
        if k == 2:
            return lax.rem(self.r + 2, 4)
        return 3 - self.r

    def plane(self, k):
        return (self.plane_index(k), self.z, self.s)


def greet(me):
    barrier = pltpu.get_barrier_semaphore()
    others = [me.core()] + [me.line(i) for i in (1, 2, 3)] + [me.plane(k) for k in (1, 2, 3)]
    for other in others:
        pl.semaphore_signal(barrier, inc=1, device_id=other, device_id_type=MESH)
    pl.semaphore_wait(barrier, len(others))


def remote(src, dst, send_sem, recv_sem, device):
    return pltpu.make_async_remote_copy(
        src_ref=src, dst_ref=dst, send_sem=send_sem, recv_sem=recv_sem, device_id=device, device_id_type=MESH
    )


def rows_of(index, count, unit=16):
    return pl.ds(pl.multiple_of(index * count, unit), count)


class Gather:
    def __init__(self, me, shards, sems):
        self.me, self.shards = me, shards
        self.zs, self.zr, self.ps, self.pr, self.fs, self.fr, self.ls = sems

    def only(self, w, cond):
        return (lambda f: pl.when(cond)(f)) if self.shards[w][2] == 2 else (lambda f: f())

    def slot(self, w, index):
        return index % 2 if self.shards[w][2] == 2 else index

    def quarter(self, w, r):
        return rows_of(r, self.shards[w][0].shape[0] // 4)

    def part(self, w, frm, r, half=None):
        dst = self.shards[w][1]
        count, cols = dst.shape[1] // 4, dst.shape[2]
        slot = self.slot(w, frm)
        if half is None:
            return dst.at[slot, rows_of(r, count)]
        if cols == 768:
            return dst.at[slot, rows_of(r, count), pl.ds(half * 384, 384)]
        return dst.at[slot, rows_of(2 * r + half, count // 2)]

    def send(self, ws):
        me = self.me
        for w in ws:
            src, dst, count = self.shards[w]

            @self.only(w, me.z // 2 == me.c)
            def _():
                for d in (2, 1, 3):
                    self.line_copy(w, d).start()
                pltpu.make_async_copy(src, dst.at[self.slot(w, me.z)], self.ls.at[w]).start()

    def line_copy(self, w, d):
        me = self.me
        return remote(
            self.shards[w][0].at[self.quarter(w, me.r)],
            self.part(w, me.z, me.r),
            self.zs.at[w, d - 1],
            self.zr.at[w, d - 1],
            me.line(d),
        )

    def plane_copy(self, w, d, k):
        me = self.me
        ref = self.part(w, me.line_index(-d), me.r)
        return remote(ref, ref, self.ps.at[w, d - 1, k - 1], self.pr.at[w, d - 1, k - 1], me.plane(k))

    def on_copy(self, w, d, k):
        me = self.me
        ref = self.part(w, me.line_index(-d), me.plane_index(3 - k), k - 1)
        return remote(ref, ref, self.fs.at[w, d - 1, k - 1], self.fr.at[w, d - 1, k - 1], me.plane(k))

    def each(self, ws, step):
        for w in ws:
            for d in (1, 2, 3):

                @self.only(w, self.me.line_index(-d) // 2 == self.me.c)
                def _():
                    step(w, d)

    def to_plane(self, ws):
        def step(w, d):
            self.line_copy(w, d).wait_recv()
            self.plane_copy(w, d, 1).start()
            self.plane_copy(w, d, 2).start()

        self.each(ws, step)

    def onward(self, ws):
        def step(w, d):
            for k in (1, 2):
                self.plane_copy(w, d, k).wait_recv()
                self.on_copy(w, d, 3 - k).start()

        self.each(ws, step)

    def ready(self, ws):
        def step(w, d):
            for k in (1, 2):
                self.on_copy(w, d, k).wait_recv()

        self.each(ws, step)
        for w in ws:
            src, dst, count = self.shards[w]

            @self.only(w, self.me.z // 2 == self.me.c)
            def _():
                pltpu.make_async_copy(src, dst.at[0], self.ls.at[w]).wait()

    def drain(self, ws):
        def step(w, d):
            for k in (1, 2):
                self.plane_copy(w, d, k).wait_send()
                self.on_copy(w, d, k).wait_send()

        self.each(ws, step)
        for w in ws:

            @self.only(w, self.me.z // 2 == self.me.c)
            def _():
                for d in (1, 2, 3):
                    self.line_copy(w, d).wait_send()


HALVES, LINE, SPREAD = 0, 1, 2


class Reduce:
    def __init__(self, me, grads, outs, bufs, sems):
        self.me, self.grads, self.outs = me, grads, outs
        self.RA, self.RB, self.RC, self.RD, self.RZ, self.SUM = bufs
        (self.as_, self.ar, self.bs, self.br, self.zs, self.zr, self.gs, self.gr, self.fs, self.fr, self.ls,
         self.cs, self.cr, self.ns, self.nr) = sems
        self.mx, self.my = lax.rem(me.r, 2), me.r // 2
        self.owner = me.z // 2 == me.c

    def kind(self, w):
        return {4: 1, 2: 0, 1: 2}[self.grads[w].shape[0]]

    def quarter(self, w):
        return self.grads[w].shape[1] // 4

    def piece(self, w, t, half):
        g = self.grads[w]
        q, cols = self.quarter(w), g.shape[2]
        if cols == 384:
            return g.at[:, rows_of(2 * t + half, q // 2)]
        return g.at[:, rows_of(t, q), pl.ds(half * (cols // 2), cols // 2)]

    def first_copy(self, w, half, other):
        if half == 0:
            t, k, land = 2 * other + 1 - self.mx, 1, self.RA
        else:
            t, k, land = 2 * (1 - self.my) + other, 2, self.RB
        i = 2 * half + other
        return remote(
            self.piece(w, t, half), land[w].at[other], self.as_.at[w, i], self.ar.at[w, i], self.me.plane(k)
        )

    def start(self, ws):
        for w in ws:
            for other in (0, 1):
                for half in (0, 1):
                    self.first_copy(w, half, other).start()

    def kept(self, w, half, other):
        t = 2 * other + self.mx if half == 0 else 2 * self.my + other
        return self.piece(w, t, half)

    def second_copy(self, w, half):
        if half == 0:
            return remote(
                self.piece(w, 2 * (1 - self.my) + self.mx, 0), self.RC[w], self.bs.at[w, 0], self.br.at[w, 0], self.me.plane(2)
            )
        return remote(
            self.piece(w, 2 * self.my + 1 - self.mx, 1), self.RD[w], self.bs.at[w, 1], self.br.at[w, 1], self.me.plane(1)
        )

    def add_into(self, target, *more):
        total = target[...].astype(F32)
        for ref in more:
            total = total + ref[...].astype(F32)
        target[...] = total.astype(BF)

    def second(self, ws):
        for w in ws:
            for other in (0, 1):
                for half in (0, 1):
                    self.first_copy(w, half, other).wait()
            for half, land in ((0, self.RA), (1, self.RB)):

                @pl.loop(0, 2)
                def _(other):
                    self.add_into(self.kept(w, half, other), land[w].at[other])

                self.second_copy(w, half).start()

    def along(self, ws):
        me = self.me
        for w in ws:
            for half, land in ((0, self.RC), (1, self.RD)):
                self.second_copy(w, half).wait()
                self.add_into(self.piece(w, me.r, half), land[w])
            if self.kind(w) == 0:
                for u in range(2):

                    @pl.when(2 * me.c + u != me.z)
                    def _():
                        self.unit_copy(w, u).start()

            else:
                for d in (1, 2, 3):
                    self.line_copy(w, d).start()

    def unit_copy(self, w, u):
        me = self.me
        target = 2 * me.c + u
        slot = lax.rem(target - me.z + 3, 4)
        slot = jnp.minimum(slot, 2)
        return remote(
            self.grads[w].at[u, rows_of(me.r, self.quarter(w))],
            self.RZ[w].at[slot],
            self.zs.at[w, u],
            self.zr.at[w, slot],
            (me.r, target, me.s),
        )

    def line_copy(self, w, d):
        me = self.me
        q = self.quarter(w)
        if self.kind(w) == 1:
            src = self.grads[w].at[me.line_index(d), rows_of(me.r, q)]
        else:
            src = self.grads[w].at[0, rows_of(me.r * 4 + me.line_index(d), q // 4)]
        return remote(src, self.RZ[w].at[d - 1], self.zs.at[w, d - 1], self.zr.at[w, d - 1], me.line(d))

    def near_copy(self, w, d):
        mine = self.SUM[w].at[rows_of(self.me.z, self.quarter(w) // 4)]
        return remote(mine, mine, self.ns.at[w - 8, d - 1], self.nr.at[w - 8, d - 1], self.me.line(d))

    def out(self, w):
        return self.outs[w].at[0] if self.kind(w) == 2 else self.outs[w]

    def out_part(self, w, t, half=None):
        out, q = self.out(w), self.quarter(w)
        cols = out.shape[1]
        if half is None:
            return out.at[rows_of(t, q)]
        if cols == 384:
            return out.at[rows_of(2 * t + half, q // 2)]
        return out.at[rows_of(t, q), pl.ds(half * (cols // 2), cols // 2)]

    def plane_copy(self, w, k):
        me = self.me
        return remote(self.SUM[w], self.out_part(w, me.r), self.gs.at[w, k - 1], self.gr.at[w, k - 1], me.plane(k))

    def on_copy(self, w, k):
        ref = self.out_part(w, self.me.plane_index(3 - k), k - 1)
        return remote(ref, ref, self.fs.at[w, k - 1], self.fr.at[w, k - 1], self.me.plane(k))

    def own_copy(self, w):
        return pltpu.make_async_copy(self.SUM[w], self.out_part(w, self.me.r), self.ls.at[w])

    def core_copy(self, w):
        if self.kind(w) == 2:
            return remote(self.outs[w].at[0], self.outs[w].at[1], self.cs.at[w], self.cr.at[w], self.me.core())
        return remote(self.outs[w], self.outs[w], self.cs.at[w], self.cr.at[w], self.me.core())

    def only(self, w):
        return (lambda f: pl.when(self.owner)(f)) if self.kind(w) == 0 else (lambda f: f())

    def spread_start(self, w):
        self.own_copy(w).start()
        self.plane_copy(w, 1).start()
        self.plane_copy(w, 2).start()

    def spread(self, ws):
        me = self.me
        for w in ws:
            q = self.quarter(w)
            if self.kind(w) == 0:
                for u in range(2):

                    @pl.when(2 * me.c + u != me.z)
                    def _():
                        self.unit_copy(w, u).wait_send()

                @pl.when(self.owner)
                def _():
                    for d in (1, 2, 3):
                        remote(self.RZ[w].at[0], self.RZ[w].at[d - 1], self.zs.at[w, 0], self.zr.at[w, d - 1], me.core()).wait_recv()
                    own = self.grads[w].at[me.z % 2, rows_of(me.r, q)]
                    self.SUM[w][...] = add_up([own] + [self.RZ[w].at[d] for d in range(3)]).astype(BF)
                    self.spread_start(w)

                continue
            for d in (1, 2, 3):
                self.line_copy(w, d).wait()
            if self.kind(w) == 1:
                own = self.grads[w].at[me.z, rows_of(me.r, q)]
                self.SUM[w][...] = add_up([own] + [self.RZ[w].at[d] for d in range(3)]).astype(BF)
                self.spread_start(w)
            else:
                own = self.grads[w].at[0, rows_of(me.r * 4 + me.z, q // 4)]
                total = add_up([own] + [self.RZ[w].at[d] for d in range(3)]).astype(BF)
                self.SUM[w][rows_of(me.z, q // 4)] = total
                for d in (1, 2, 3):
                    self.near_copy(w, d).start()

    def spread_near(self, ws):
        for w in ws:
            for d in (1, 2, 3):
                self.near_copy(w, d).wait()
            self.spread_start(w)

    def onward(self, ws):
        for w in ws:

            @self.only(w)
            def _():
                for k in (1, 2):
                    self.plane_copy(w, k).wait()
                    self.on_copy(w, 3 - k).start()

    def finish(self, ws):
        for w in ws:

            @self.only(w)
            def _():
                self.own_copy(w).wait()
                for k in (1, 2):
                    self.on_copy(w, k).wait()
                if self.kind(w) != 1:
                    self.core_copy(w).start()

    def end(self, ws):
        for w in ws:
            if self.kind(w) == 0:

                @pl.when(self.owner)
                def _():
                    self.core_copy(w).wait_send()

                @pl.when(jnp.logical_not(self.owner))
                def _():
                    self.core_copy(w).wait_recv()

            elif self.kind(w) == 2:
                self.core_copy(w).wait()


def add_up(refs):
    total = refs[0][...].astype(F32)
    for ref in refs[1:]:
        total = total + ref[...].astype(F32)
    return total


def nn(a, b):
    return lax.dot_general(a, b, (((1,), (0,)), ((), ())), preferred_element_type=F32)


def nt(a, b):
    return lax.dot_general(a, b, (((1,), (1,)), ((), ())), preferred_element_type=F32)


def tn(a, b):
    return lax.dot_general(a, b, (((0,), (0,)), ((), ())), preferred_element_type=F32)


def norm_parts(value):
    center = value - jnp.mean(value, axis=-1, keepdims=True)
    spread = jnp.mean(center * center, axis=-1, keepdims=True)
    rstd = lax.rsqrt(spread + EPS)
    return center * rstd, rstd


def norm_grad(xh, rstd, gain, dy):
    scaled = dy * gain
    mean_one = jnp.mean(scaled, axis=-1, keepdims=True)
    mean_two = jnp.mean(scaled * xh, axis=-1, keepdims=True)
    return (scaled - mean_one - xh * mean_two) * rstd


def col_sum(value):
    return jnp.sum(value, axis=0, keepdims=True)


class Swap:
    def __init__(self, me, send, recv, ssem, rsem, chunks):
        self.me, self.send, self.recv, self.ssem, self.rsem = me, send, recv, ssem, rsem
        self.rows = send.shape[1] // chunks
        self.chunks = chunks
        self.turn = 0

    def copy(self, slot, i):
        rows = rows_of(i, self.rows)
        return remote(
            self.send.at[slot, rows],
            self.recv.at[slot, rows],
            self.ssem.at[slot, i],
            self.rsem.at[slot, i],
            self.me.core(),
        )

    def run(self, part, between, post):
        slot = self.turn % 2
        self.turn += 1

        @pl.loop(0, self.chunks)
        def _(i):
            rows = rows_of(i, self.rows)
            self.send[slot, rows] = part(rows).astype(BF)
            self.copy(slot, i).start()

        if between is not None:
            between()

        @pl.loop(0, self.chunks)
        def _(i):
            rows = rows_of(i, self.rows)
            self.copy(slot, i).wait()
            total = self.send[slot, rows].astype(F32) + self.recv[slot, rows].astype(F32)
            post(i, rows, total)


class Layer:
    def __init__(self, **kw):
        self.__dict__.update(kw)


def head_mask(layer, i, c):
    h = lax.rem(i, 3)
    half = jnp.where(h == 2, layer.third(c), lax.rem(h, 2))
    lane = lax.broadcasted_iota(jnp.int32, (1, 128), 1) // 64
    mask = jnp.where(lane == half, 1.0, 0.0).astype(BF)
    return i // 3, pl.ds(pl.multiple_of((h // 2) * 128, 128), 128), mask


def forward(layer, me, swap, bias_row, prm, hook, done):
    L, c = layer, me.c
    units = L.q.shape[0]

    hook("qkv")
    project = nt if L.flip_attn else nn

    @pl.loop(0, units)
    def _(u):
        x = L.x[...]
        n = L.width
        L.q[u, :, :n] = ((project(x, L.wq[u]) + L.bias_q(u)).astype(BF) * 0.125).astype(BF)
        L.k[u, :, :n] = project(x, L.wk[u]).astype(BF)
        L.v[u, :, :n] = (project(x, L.wv[u]) + L.bias_v(u)).astype(BF)
        if n < 256:
            pad = jnp.zeros((x.shape[0], 256 - n), BF)
            L.q[u, :, n:] = pad
            L.k[u, :, n:] = pad
            L.v[u, :, n:] = pad
        L.o[u] = jnp.zeros(L.o.shape[1:], BF)

    hook("heads")

    def heads(lo, hi):
        @pl.loop(lo, hi)
        def _(i):
            u, cols, mask = head_mask(L, i, c)
            k = L.k[u, :, cols]
            v = L.v[u, :, cols] * mask
            for ch in range(4):
                rows = pl.ds(ch * 128, 128)
                scores = nt(L.q[u, rows, cols] * mask, k) + bias_row[0:1, :]
                top = jnp.max(scores, axis=-1, keepdims=True)
                expo = jnp.exp(scores - top)
                inv = 1.0 / jnp.sum(expo, axis=-1, keepdims=True)
                probs = (expo * inv).astype(BF)
                L.p[i, rows] = probs
                L.o[u, rows, cols] = L.o[u, rows, cols] + nn(probs, v).astype(BF)

    heads(0, 3)
    if units == 2:
        hook("middle")
        heads(3, 6)
    hook("attn")

    def attn_part(rows):
        n = L.width
        total = nn(L.o[0, rows, :n], L.wo[0])
        for u in range(1, units):
            total = total + nn(L.o[u, rows, :n], L.wo[u])
        return total

    def attn_post(i, rows, total):
        value = L.x[rows].astype(F32) + total + prm[L.prow : L.prow + 1, :]
        xh, rstd = norm_parts(value)
        L.xh1[rows] = xh
        L.rs1[rows] = rstd
        L.a[rows] = (xh * prm[L.prow + 1 : L.prow + 2, :] + prm[L.prow + 2 : L.prow + 3, :]).astype(BF)

    swap.run(attn_part, None, attn_post)
    hook("ffn_in")
    enter = nt if L.flip_in else nn

    @pl.loop(0, 4)
    def _(j):
        pre = enter(L.a[...], L.wi[j]) + L.bias_i(j)
        sq = pre * pre
        t = jnp.tanh(0.7978845608028654 * pre * (1.0 + 0.044715 * sq))
        half = 0.5 * (1.0 + t)
        L.g[j] = (pre * half).astype(BF)
        slope = half + 0.5 * pre * (1.0 - t * t) * (0.7978845608028654 + 0.7978845608028654 * 0.134145 * sq)
        L.gp[j] = slope.astype(BF)

    hook("ffn_out")

    def ffn_part(rows):
        total = nn(L.g[0, rows], L.wf[0])
        for j in range(1, 4):
            total = total + nn(L.g[j, rows], L.wf[j])
        return total

    def ffn_post(i, rows, total):
        value = L.a[rows].astype(F32) + total + prm[L.prow + 3 : L.prow + 4, :]
        xh, rstd = norm_parts(value)
        L.xh2[rows] = xh
        L.rs2[rows] = rstd
        done(rows, xh * prm[L.prow + 4 : L.prow + 5, :] + prm[L.prow + 5 : L.prow + 6, :])

    swap.run(ffn_part, None, ffn_post)


def backward(layer, me, swap, prm, sums, upstream, hook, done):
    L, c = layer, me.c
    units = L.q.shape[0]
    prow = L.prow
    n_rows = L.x.shape[0]
    for i in range(6):
        sums[prow + i : prow + i + 1, :] = jnp.zeros((1, 768), F32)

    @pl.loop(0, n_rows // 128)
    def _(i):
        rows = rows_of(i, 128)
        dy = upstream(rows)
        xh = L.xh2[rows]
        sums[prow + 4 : prow + 5, :] += col_sum(dy * xh)
        sums[prow + 5 : prow + 6, :] += col_sum(dy)
        df = norm_grad(xh, L.rs2[rows], prm[prow + 4 : prow + 5, :], dy)
        low = df.astype(BF)
        sums[prow + 3 : prow + 4, :] += col_sum(low.astype(F32))
        L.df[rows] = df
        L.dr[rows] = low

    @pl.loop(0, 4)
    def _(j):
        dpre = (nt(L.dr[...], L.wf[j]) * L.gp[j].astype(F32)).astype(BF)
        L.gp[j] = dpre
        n = dpre.shape[1]
        sums[pl.ds(L.brow + j, 1), :n] = col_sum(dpre.astype(F32))

    leave = nn if L.flip_in else nt

    def ffn_part(rows):
        total = leave(L.gp[0, rows], L.wi[0])
        for j in range(1, 4):
            total = total + leave(L.gp[j, rows], L.wi[j])
        return total

    def ffn_weights():
        @pl.loop(0, 4)
        def _(j):
            L.wf[j] = tn(L.g[j], L.dr[...]).astype(BF)
            if L.flip_in:
                L.wi[j] = tn(L.gp[j], L.a[...]).astype(BF)
            else:
                L.wi[j] = tn(L.a[...], L.gp[j]).astype(BF)

        hook("ffn_grads")

    def ffn_post(i, rows, total):
        da = L.df[rows] + total
        xh = L.xh1[rows]
        sums[prow + 1 : prow + 2, :] += col_sum(da * xh)
        sums[prow + 2 : prow + 3, :] += col_sum(da)
        dh = norm_grad(xh, L.rs1[rows], prm[prow + 1 : prow + 2, :], da)
        low = dh.astype(BF)
        sums[prow : prow + 1, :] += col_sum(low.astype(F32))
        L.df[rows] = dh
        L.dr[rows] = low

    swap.run(ffn_part, ffn_weights, ffn_post)
    hook("attn")

    @pl.loop(0, units)
    def _(u):
        n = L.width
        L.do[u, :, :n] = nt(L.dr[...], L.wo[u]).astype(BF)
        if n < 256:
            L.do[u, :, n:] = jnp.zeros((n_rows, 256 - n), BF)
        for ref in (L.dq, L.dk, L.dv):
            ref[u] = jnp.zeros(ref.shape[1:], BF)

    @pl.loop(0, 3 * units)
    def _(i):
        u, cols, mask = head_mask(L, i, c)
        k = L.k[u, :, cols] * mask
        v = L.v[u, :, cols]
        for ch in range(4):
            rows = pl.ds(ch * 128, 128)
            d_probs = nt(L.do[u, rows, cols] * mask, v)
            probs = L.p[i, rows].astype(F32)
            both = probs * d_probs
            d_scores = (both - probs * jnp.sum(both, axis=-1, keepdims=True)).astype(BF)
            L.ds[rows] = d_scores
            L.dq[u, rows, cols] = L.dq[u, rows, cols] + (nn(d_scores, k) * 0.125).astype(BF)
        L.dv[u, :, cols] = L.dv[u, :, cols] + tn(L.p[i], L.do[u, :, cols] * mask).astype(BF)
        L.dk[u, :, cols] = L.dk[u, :, cols] + tn(L.ds[...], L.q[u, :, cols] * mask).astype(BF)

    hook("heads_done")
    back = nn if L.flip_attn else nt

    def attn_part(rows):
        n = L.width
        total = None
        for u in range(units):
            for grad, weight in ((L.dq, L.wq), (L.dk, L.wk), (L.dv, L.wv)):
                term = back(grad[u, rows, :n], weight[u])
                total = term if total is None else total + term
        return total

    def attn_weights():
        @pl.loop(0, units)
        def _(u):
            n = L.width
            L.wo[u] = tn(L.o[u, :, :n], L.dr[...]).astype(BF)
            x = L.x[...]
            for grad, out in ((L.dq, L.wq), (L.dk, L.wk), (L.dv, L.wv)):
                out[u] = (tn(grad[u, :, :n], x) if L.flip_attn else tn(x, grad[u, :, :n])).astype(BF)
            sums[pl.ds(L.qrow + u, 1), :256] = col_sum(L.dq[u].astype(F32))
            sums[pl.ds(L.qrow + units + u, 1), :256] = col_sum(L.dv[u].astype(F32))

        hook("attn_grads")

    def attn_post(i, rows, total):
        done(rows, L.df[rows] + total)

    swap.run(attn_part, attn_weights, attn_post)


class Sequences:
    def __init__(self, me, pairs, sems):
        self.me, self.pairs = me, pairs
        self.xs, self.xr, self.fs, self.fr = sems
        self.owner = me.z // 2 == me.c

    def send(self, a):
        me = self.me
        src, dst = self.pairs[a]
        for j in range(2):
            target = 2 * me.c + j

            @pl.when(target != me.z)
            def _():
                remote(src.at[j], dst.at[rows_of(me.z, 128)], self.xs.at[a, j], self.xr.at[a, me.z], (me.r, target, me.s)).start()

            @pl.when(target == me.z)
            def _():
                pltpu.make_async_copy(src.at[j], dst.at[rows_of(me.z, 128)], self.xr.at[a, me.z]).start()

    def core_copy(self, a, frm, i):
        dst = self.pairs[a][1].at[rows_of(frm, 128)]
        return remote(dst, dst, self.fs.at[a, i], self.fr.at[a, frm], self.me.core())

    def take(self, a):
        me = self.me
        src, dst = self.pairs[a]

        @pl.when(self.owner)
        def _():
            pltpu.make_async_copy(src.at[0], dst.at[rows_of(me.z, 128)], self.xr.at[a, me.z]).wait()
            self.core_copy(a, me.z, 0).start()
            for d in (1, 2, 3):
                frm = me.line_index(-d)
                remote(src.at[0], dst.at[rows_of(frm, 128)], self.xs.at[a, 0], self.xr.at[a, frm], me.core()).wait_recv()
                self.core_copy(a, frm, d).start()

        @pl.when(jnp.logical_not(self.owner))
        def _():
            for i in range(4):
                self.core_copy(a, i, i).wait_recv()

    def drain(self, a):
        me = self.me
        src, dst = self.pairs[a]
        for j in range(2):

            @pl.when(2 * me.c + j != me.z)
            def _():
                remote(src.at[j], dst.at[rows_of(me.z, 128)], self.xs.at[a, j], self.xr.at[a, me.z], me.core()).wait_send()

        @pl.when(self.owner)
        def _():
            for i in range(4):
                self.core_copy(a, i, i).wait_send()


class Home:
    def __init__(self, me, pairs, sems):
        self.me, self.pairs = me, pairs
        self.ys, self.yr = sems
        self.owner = me.z // 2 == me.c

    def send(self, a):
        me = self.me
        src, dst = self.pairs[a]

        @pl.when(self.owner)
        def _():
            pltpu.make_async_copy(src.at[rows_of(me.z, 128)], dst.at[me.z % 2], self.yr.at[a, me.z % 2]).start()
            for d in (1, 2, 3):
                remote(
                    src.at[rows_of(me.line_index(d), 128)],
                    dst.at[me.z % 2],
                    self.ys.at[a, d - 1],
                    self.yr.at[a, me.z % 2],
                    me.line(d),
                ).start()

    def drain(self, a):
        me = self.me
        src, dst = self.pairs[a]

        @pl.when(self.owner)
        def _():
            for d in (1, 2, 3):
                remote(src.at[rows_of(0, 128)], dst.at[0], self.ys.at[a, d - 1], self.yr.at[a, 0], me.core()).wait_send()

        for j in range(2):
            chip = 2 * me.c + j

            @pl.when(chip == me.z)
            def _():
                pltpu.make_async_copy(src.at[rows_of(0, 128)], dst.at[j], self.yr.at[a, j]).wait()

            @pl.when(chip != me.z)
            def _():
                remote(src.at[rows_of(0, 128)], dst.at[j], self.ys.at[a, 0], self.yr.at[a, j], me.core()).wait_recv()


def row(ref):
    return ref[...].astype(F32).reshape(1, ref.shape[0])


def main_kernel(*refs):
    me = Place()
    z, c = me.z, me.c
    lens = refs[0]
    (tok, cot, tq, tk, tv, to, ti, tf, si, sf, SQ, SK, SV, SO) = refs[1:15]
    vectors = refs[15:27]
    sqb, svb, tqb, tvb, tib, sib = refs[27:33]
    (YO, DO, SUMS) = refs[33:36]
    outs = refs[36:48]
    rest = list(refs[48:])

    def take(count):
        head, rest[:] = rest[:count], rest[count:]
        return head

    WQ, WK, WV, WO, WI, WF, SI, SF, wsq, wsk, wsv, wso = weights = take(12)
    X, CT, LN, PACK, BP, PRM, SM, sml = take(8)
    bias_row, send, recv, ssem, rsem = take(5)
    q, k, v, o, p, xh1, rs1, a, g, gp, xh2, rs2, df, dr, do, dq, dk, dv, ds = take(19)
    x2, q2, k2, v2, o2, p2, xh12, rs12, a2, g2, gp2, xh22, rs22, dx2, Y, DX = take(16)
    bufs = [take(12) for _ in range(6)]
    gather_sems = take(7)
    reduce_sems = take(15)
    seq_sems, home_sems = take(4), take(2)
    pks, pkr, lcs, lcr, sls, sms, smr = take(7)

    LN[0] = jnp.full(LN.shape[1:], lens[z % 2].astype(F32))
    PACK[...] = jnp.zeros(PACK.shape, F32)
    PACK[0:1, 0:192] = row(tqb)
    PACK[1:2, :] = row(tib)
    PACK[2:3, 0 : sib.shape[0]] = row(sib)
    PACK[3:4, 0:192] = row(tvb)
    greet(me)
    owner = z // 2 == c

    sequences = Sequences(me, ((tok, X), (cot, CT)), seq_sems)
    home = Home(me, ((Y, YO), (DX, DO)), home_sems)
    gather = Gather(
        me,
        ((tq, WQ, 2), (tk, WK, 2), (tv, WV, 2), (to, WO, 2), (ti, WI, 4), (tf, WF, 4), (si, SI, 4), (sf, SF, 4)),
        gather_sems,
    )
    G0, G1, G2, G3 = (0, 1, 2), (3, 4), (5,), (6, 7)

    sequences.send(0)
    pack_copies = [remote(PACK, BP.at[z], pks.at[d - 1], pkr.at[d - 1], me.line(d)) for d in (1, 2, 3)]
    for copy in pack_copies:
        copy.start()
    gather.send(G0)
    gather.send(G1)
    lens_copy = remote(LN.at[0], LN.at[1], lcs.at[0], lcr.at[0], me.core())

    @pl.when(owner)
    def _():
        lens_copy.start()

    first = pl.ds(pl.multiple_of(c * 256, 128), 128)
    local = []
    for i, (src, dst) in enumerate(((SQ, wsq), (SK, wsk), (SV, wsv))):
        local.append((src.at[:, first], dst.at[0, :, pl.ds(0, 128)]))
        local.append((src.at[:, pl.ds(128, 128)], dst.at[0, :, pl.ds(128, 128)]))
    local.append((SO.at[first], wso.at[0, pl.ds(0, 128)]))
    local.append((SO.at[pl.ds(128, 128)], wso.at[0, pl.ds(128, 128)]))
    local.append((PACK, BP.at[z]))
    local = [pltpu.make_async_copy(src, dst, sls.at[i]) for i, (src, dst) in enumerate(local)]
    for copy in local:
        copy.start()
    for i, ref in enumerate(vectors):
        PRM[i : i + 1, :] = row(ref)
    PRM[12:13, 0:384] = row(sqb)
    PRM[12:13, 384:768] = row(svb)
    SM[...] = jnp.zeros(SM.shape, F32)

    @pl.when(owner)
    def _():
        lens_copy.wait_send()

    @pl.when(jnp.logical_not(owner))
    def _():
        lens_copy.wait_recv()

    n_keys = X.shape[0]
    position = lax.broadcasted_iota(jnp.int32, (8, n_keys), 1).astype(F32)
    length = jnp.where(owner, LN[0], LN[1])
    bias_row[...] = jnp.where(position < length[:, 0:1], 0.0, MASKED)
    s_bias = pl.ds(pl.multiple_of(c * 256, 128), 128)
    v_bias = pl.ds(pl.multiple_of(384 + c * 256, 128), 128)

    teacher = Layer(
        x=X, wq=WQ, wk=WK, wv=WV, wo=WO, wi=WI, wf=WF, q=q, k=k, v=v, o=o, p=p, xh1=xh1, rs1=rs1, a=a, g=g, gp=gp,
        xh2=xh2, rs2=rs2, df=df, dr=dr, do=do, dq=dq, dk=dk, dv=dv, ds=ds, prow=0, qrow=12, brow=16,
        width=192, flip_attn=True, flip_in=False,
        bias_q=lambda u: BP[2 * c + u, 0:1, 0:192],
        bias_v=lambda u: BP[2 * c + u, 3:4, 0:192],
        bias_i=lambda j: BP[j, 1:2, :],
        third=lambda c: 0,
    )
    student = Layer(
        x=x2, wq=wsq, wk=wsk, wv=wsv, wo=wso, wi=SI, wf=SF, q=q2, k=k2, v=v2, o=o2, p=p2, xh1=xh12, rs1=rs12, a=a2,
        g=g2, gp=gp2, xh2=xh22, rs2=rs22, df=df, dr=dr, do=do, dq=dq, dk=dk, dv=dv, ds=ds, prow=6, qrow=24, brow=20,
        width=256, flip_attn=False, flip_in=True,
        bias_q=lambda u: jnp.concatenate([PRM[12:13, s_bias], PRM[12:13, 128:256]], axis=1),
        bias_v=lambda u: jnp.concatenate([PRM[12:13, v_bias], PRM[12:13, 512:640]], axis=1),
        bias_i=lambda j: BP[j, 2:3, 0 : SI.shape[1]],
        third=lambda c: c,
    )
    swap = Swap(me, send, recv, ssem, rsem, 4)

    def teacher_hook(name):
        if name == "qkv":
            sequences.take(0)
            gather.to_plane(G0)
            gather.onward(G0)
            gather.to_plane(G1[:1])
            for copy in pack_copies:
                copy.wait()
            for copy in local:
                copy.wait()
            gather.ready(G0)
        if name == "heads":
            gather.send(G2)
            gather.onward(G1[:1])
            gather.to_plane(G1[1:])
        if name == "middle":
            gather.onward(G1[1:])
            gather.send(G3)
            gather.to_plane(G2)
        if name == "attn":
            gather.onward(G2)
            gather.to_plane(G3)
            sequences.send(1)
            gather.ready(G1[:1])
        if name == "ffn_in":
            gather.ready(G1[1:])
        if name == "ffn_out":
            gather.onward(G3)
            gather.ready(G2)

    def student_hook(name):
        if name == "ffn_in":
            gather.ready(G3)
            sequences.take(1)

    def to_student(rows, value):
        x2[rows] = value.astype(BF)

    def to_output(rows, value):
        Y[rows] = value.astype(BF)

    def between(rows, value):
        dx2[rows] = value

    def to_grad(rows, value):
        DX[rows] = value.astype(BF)

    forward(teacher, me, swap, bias_row, PRM, teacher_hook, to_student)
    forward(student, me, swap, bias_row, PRM, student_hook, to_output)
    home.send(0)
    gather.drain(range(8))
    sequences.drain(0)
    sequences.drain(1)

    total = Reduce(me, weights, outs, bufs, reduce_sems)
    R0, R1, R2, R3 = (6, 7), (8, 9, 10, 11), (4, 5), (0, 1, 2, 3)

    def student_back(name):
        if name == "ffn_grads":
            total.start(R0)
        if name == "attn_grads":
            total.start(R1)

    def teacher_back(name):
        if name == "ffn_grads":
            total.start(R2)
            total.second(R0)
            total.second(R1)
        if name == "heads_done":
            total.along(R0)
            total.along(R1)
        if name == "attn_grads":
            total.start(R3)

    backward(student, me, swap, PRM, SM, lambda rows: CT[rows].astype(F32), student_back, between)
    backward(teacher, me, swap, PRM, SM, lambda rows: dx2[rows], teacher_back, to_grad)
    home.send(1)

    sml[0] = SM[...]
    for d in (1, 2, 3):
        remote(sml.at[0], sml.at[d], sms.at[d - 1], smr.at[d - 1], me.line(d)).start()
    total.spread(R0)
    total.spread(R1)
    total.second(R2)
    total.second(R3)
    total.spread_near(R1)
    for d in (1, 2, 3):
        remote(sml.at[0], sml.at[d], sms.at[d - 1], smr.at[d - 1], me.line(d)).wait()
    sml[4] = add_up([sml.at[i] for i in range(4)])
    for k in (1, 2, 3):
        remote(sml.at[4], sml.at[4 + k], sms.at[2 + k], smr.at[2 + k], me.plane(k)).start()
    total.onward(R0)
    total.along(R2)
    total.along(R3)
    total.onward(R1)
    for k in (1, 2, 3):
        remote(sml.at[4], sml.at[4 + k], sms.at[2 + k], smr.at[2 + k], me.plane(k)).wait()
    sml[8] = add_up([sml.at[4 + i] for i in range(4)])
    other_sums = remote(sml.at[8], sml.at[9], sms.at[6], smr.at[6], me.core())
    other_sums.start()
    total.spread(R2)
    total.finish(R0)
    total.finish(R1)
    total.spread(R3)
    total.onward(R2)
    total.onward(R3)
    other_sums.wait()
    both_sums = pltpu.make_async_copy(sml.at[pl.ds(8, 2)], SUMS, sls.at[9])
    both_sums.start()
    total.finish(R2)
    total.finish(R3)
    total.end(R1)
    total.end(R3)
    home.drain(0)
    home.drain(1)
    both_sums.wait()


def final_kernel(*refs):
    z = lax.axis_index("head")
    c = lax.rem(lax.axis_index("seq"), 2)
    YO, DO, SUMS = refs[:3]
    grads = refs[3:15]
    outs = refs[15:]
    outs[0][...] = YO[...].astype(F32)
    outs[1][...] = DO[...].astype(F32)
    for at, w in ((2, 0), (4, 1), (5, 2), (7, 3), (11, 4), (13, 5), (26, 6), (28, 7)):
        outs[at][...] = grads[w][...].astype(F32)
    near = pl.ds(pl.multiple_of(c * 256, 128), 128)
    far = pl.ds(pl.multiple_of((1 - c) * 256, 128), 128)
    for at, w in ((17, 8), (19, 9), (20, 10)):
        g = grads[w]
        outs[at][:, near] = g[0, :, 0:128].astype(F32)
        outs[at][:, far] = g[1, :, 0:128].astype(F32)
        outs[at][:, 128:256] = g[0, :, 128:256].astype(F32) + g[1, :, 128:256].astype(F32)
    g = grads[11]
    outs[22][near, :] = g[0, 0:128, :].astype(F32)
    outs[22][far, :] = g[1, 0:128, :].astype(F32)
    outs[22][128:256, :] = g[0, 128:256, :].astype(F32) + g[1, 128:256, :].astype(F32)

    def put(at, value):
        outs[at][...] = value.reshape(value.shape[1])

    for i, at in enumerate((8, 9, 10, 14, 15, 16, 23, 24, 25, 29, 30, 31)):
        put(at, SUMS[0, i : i + 1, :])
    side = jnp.where(z // 2 == c, 0, 1)
    put(3, SUMS[side, pl.ds(12 + z % 2, 1), 0:192])
    put(6, SUMS[side, pl.ds(14 + z % 2, 1), 0:192])
    put(12, SUMS[0, pl.ds(16 + z, 1), 0 : outs[12].shape[0]])
    put(27, SUMS[0, pl.ds(20 + z, 1), 0 : outs[27].shape[0]])
    for at, r in ((18, 24), (21, 25)):
        low = jnp.where(c == 0, SUMS[0, r : r + 1, 0:128], SUMS[1, r : r + 1, 0:128])
        high = jnp.where(c == 0, SUMS[1, r : r + 1, 0:128], SUMS[0, r : r + 1, 0:128])
        middle = SUMS[0, r : r + 1, 128:256] + SUMS[1, r : r + 1, 128:256]
        put(at, jnp.concatenate([low, middle, high], axis=1))


ANYWHERE = pl.BlockSpec(memory_space=pl.ANY)
IN_VMEM = pl.BlockSpec(memory_space=pltpu.VMEM)


def shape(*dims, kind=BF):
    return jax.ShapeDtypeStruct(dims, kind)


def body(
    tokens, lengths, cotangent,
    t_query, t_query_bias, t_key, t_value, t_value_bias, t_attn_out, t_attn_bias, t_norm1_gain, t_norm1_bias,
    t_ffn_in, t_ffn_in_bias, t_ffn_out, t_ffn_out_bias, t_norm2_gain, t_norm2_bias,
    s_query, s_query_bias, s_key, s_value, s_value_bias, s_attn_out, s_attn_bias, s_norm1_gain, s_norm1_bias,
    s_ffn_in, s_ffn_in_bias, s_ffn_out, s_ffn_out_bias, s_norm2_gain, s_norm2_bias,
):
    seq_size = lax.axis_size("seq")
    outer = seq_size // 2
    groups = [[2 * y + core for y in range(outer)] for core in range(2)]

    def widen(value, axis):
        if outer == 1:
            return value
        return lax.all_gather(value, "seq", axis=axis, tiled=True, axis_index_groups=groups)

    t_ffn_in, t_ffn_in_bias, t_ffn_out = widen(t_ffn_in, 1), widen(t_ffn_in_bias, 0), widen(t_ffn_out, 0)
    s_ffn_in, s_ffn_in_bias, s_ffn_out = widen(s_ffn_in, 1), widen(s_ffn_in_bias, 0), widen(s_ffn_out, 0)
    n_in, n_s = t_ffn_in.shape[1], s_ffn_in.shape[1]
    n = 4 * tokens.shape[1]

    dma = pltpu.SemaphoreType.DMA
    act = lambda *dims, kind=BF: pltpu.VMEM(dims, kind)
    wide = lambda *dims: pltpu.VMEM(dims, F32)
    weights = [
        (2, 192, 768), (2, 192, 768), (2, 192, 768), (2, 192, 768),
        (4, 768, n_in), (4, n_in, 768), (4, n_s, 768), (4, n_s, 768),
        (1, 768, 256), (1, 768, 256), (1, 768, 256), (1, 256, 768),
    ]
    names = len(weights)

    def piece(w):
        count, rows, cols = weights[w]
        return (count, rows // 8, cols) if cols == 384 else (count, rows // 4, cols // 2)

    def share(w):
        count, rows, cols = weights[w]
        return (rows // 16 if count == 1 else rows // 4, cols)

    results = pl.pallas_call(
        main_kernel,
        out_shape=[shape(2, 128, 768), shape(2, 128, 768), shape(2, 32, 768, kind=F32)]
        + [shape(2, *d[1:]) if d[0] == 1 else shape(*d[1:]) for d in weights],
        in_specs=[pl.BlockSpec(memory_space=pltpu.SMEM)] + [ANYWHERE] * 14 + [IN_VMEM] * 18,
        out_specs=[ANYWHERE] * (3 + names),
        scratch_shapes=[act(*d) for d in weights]
        + [
            act(n, 768), act(n, 768), wide(2, 8, 128), wide(8, n_in), wide(4, 8, n_in), wide(16, 768), wide(32, 768), wide(10, 32, 768),
            wide(8, n), act(2, n, 768), act(2, n, 768), dma((2, 4)), dma((2, 4)),
            act(2, n, 256), act(2, n, 256), act(2, n, 256), act(2, n, 256), act(6, n, n),
            wide(n, 768), wide(n, 1), act(n, 768), act(4, n, n_in), act(4, n, n_in), wide(n, 768), wide(n, 1),
            wide(n, 768), act(n, 768), act(2, n, 256), act(2, n, 256), act(2, n, 256), act(2, n, 256), act(n, n),
            act(n, 768), act(1, n, 256), act(1, n, 256), act(1, n, 256), act(1, n, 256), act(3, n, n),
            wide(n, 768), wide(n, 1), act(n, 768), act(4, n, n_s), act(4, n, n_s), wide(n, 768), wide(n, 1),
            wide(n, 768), act(n, 768), act(n, 768),
        ]
        + [act(2, *piece(w)) for w in range(names)]
        + [act(2, *piece(w)) for w in range(names)]
        + [act(*piece(w)) for w in range(names)]
        + [act(*piece(w)) for w in range(names)]
        + [act(3, *share(w)) for w in range(names)]
        + [act(weights[w][1] // 4, weights[w][2]) for w in range(names)]
        + [
            dma((8, 3)), dma((8, 3)), dma((8, 3, 2)), dma((8, 3, 2)), dma((8, 3, 2)), dma((8, 3, 2)), dma((8,)),
            dma((names, 4)), dma((names, 4)), dma((names, 2)), dma((names, 2)), dma((names, 3)), dma((names, 3)),
            dma((names, 2)), dma((names, 2)), dma((names, 2)), dma((names, 2)), dma((names,)), dma((names,)), dma((names,)),
            dma((4, 3)), dma((4, 3)),
            dma((2, 2)), dma((2, 4)), dma((2, 4)), dma((2, 4)), dma((2, 3)), dma((2, 2)),
            dma((3,)), dma((3,)), dma((1,)), dma((1,)), dma((10,)), dma((7,)), dma((7,)),
        ],
        compiler_params=pltpu.CompilerParams(collective_id=0, has_side_effects=True, vmem_limit_bytes=VMEM_LIMIT),
        name="layers",
    )(
        lengths, tokens, cotangent, t_query.T, t_key.T, t_value.T, t_attn_out, t_ffn_in, t_ffn_out, s_ffn_in.T, s_ffn_out,
        s_query, s_key, s_value, s_attn_out,
        t_attn_bias, t_norm1_gain, t_norm1_bias, t_ffn_out_bias, t_norm2_gain, t_norm2_bias,
        s_attn_bias, s_norm1_gain, s_norm1_bias, s_ffn_out_bias, s_norm2_gain, s_norm2_bias,
        s_query_bias, s_value_bias, t_query_bias, t_value_bias, t_ffn_in_bias, s_ffn_in_bias,
    )
    results = list(results)

    if outer > 1:
        results[2] = lax.psum(results[2], "seq", axis_index_groups=groups)
        results[3:] = [lax.psum(g.astype(F32), "seq", axis_index_groups=groups).astype(BF) for g in results[3:]]

    f = functools.partial(shape, kind=F32)
    final_shapes = [
        f(2, 128, 768), f(2, 128, 768),
        f(192, 768), f(192), f(192, 768), f(192, 768), f(192), f(192, 768),
        f(768), f(768), f(768), f(768, n_in), f(n_in), f(n_in, 768), f(768), f(768), f(768),
        f(768, 384), f(384), f(768, 384), f(768, 384), f(384), f(384, 768),
        f(768), f(768), f(768), f(n_s, 768), f(n_s), f(n_s, 768), f(768), f(768), f(768),
    ]
    outs = list(
        pl.pallas_call(
            final_kernel,
            out_shape=final_shapes,
            in_specs=[IN_VMEM] * (3 + names),
            out_specs=[IN_VMEM] * len(final_shapes),
            compiler_params=pltpu.CompilerParams(vmem_limit_bytes=VMEM_LIMIT),
            name="final",
        )(*results)
    )
    for i in (2, 4, 5, 26):
        outs[i] = outs[i].T
    if outer > 1:
        y = lax.axis_index("seq") // 2
        for i, axis in ((11, 1), (12, 0), (13, 0), (26, 1), (27, 0), (28, 0)):
            width = outs[i].shape[axis] // outer
            outs[i] = lax.dynamic_slice_in_dim(outs[i], y * width, width, axis)
    return tuple(outs)


def solution(mesh):
    seqs = P(("row", "seq"), "head", None)
    col, line, row_spec = P(None, "head"), P("head"), P("head", None)
    fcol, fline, frow = P(None, ("head", "seq")), P(("head", "seq")), P(("head", "seq"), None)
    rep = P()
    teacher = (col, line, col, col, line, row_spec, rep, rep, rep, fcol, fline, frow, rep, rep, rep)
    student = (rep,) * 9 + (fcol, fline, frow, rep, rep, rep)
    return jax.shard_map(
        body,
        mesh=mesh,
        in_specs=(seqs, P(("row", "seq")), seqs) + teacher + student,
        out_specs=(seqs, seqs) + teacher + student,
        check_vma=False,
    )
```

time: 550 us -> 273 us (0.50)
  Pallas kernels: 500 us -> 272 us
  other arithmetic: 22 us -> 0 us
  local copies, waits for them, and re-layouts: 21.9 us -> 0 us
    pallas_call x3 -> x1, Pallas kernels: 492 us -> 264 us  [body(): pl.pallas_call(main_kernel, out_shape=[shape(2, 128, 768), shape(2, 128,...]
    pallas_call x15 -> x0, other arithmetic: 19.3 us -> none  [body(): pl.pallas_call(final_kernel, out_shape=final_shapes, in_specs=[IN_VMEM] *...]
    unnamed x20 -> x0, local copies, waits for them, and re-layouts: 10.1 us -> none
    another operation x18 -> x0, local copies, waits for them, and re-layouts: 9.1 us -> none  [the longest x14 8.4 us: body(): jnp.stack([t_attn_bias, t_norm1_gain, t_norm1_bias, t_ffn_out_bias, t_nor...]
where the time goes in v2:
time: 273 us
  Pallas kernels  272 us (100%)
    pallas_call x1, Pallas kernels, body(): pl.pallas_call(main_kernel, out_shape=[shape(2, 128, 768), shape(2, 128,...  264 us
    pallas_call x1, Pallas kernels, body(): pl.pallas_call(final_kernel, out_shape=final_shapes, in_specs=[IN_VMEM] *...  8.08 us

profile of v2, /device:TPU:0, one launch (start us, length us, event | category | flops | bytes accessed | tf_op | source)
XLA Modules:
  0.0 272.6 jit_solution(8745475455783233597)
XLA Ops:
  0.7 263.7 %layers.1 = (bf16[2,128,768]{2,1,0:T(8,128)(2,1)}, bf16[2,128,768]{2,1,0:T(8,128)(2,1)}, f32[2,32,768]{2,1,0:T(8,128)}, bf16[192,768]{1,0:T(8,128)(2,1)}, bf16[1...) custom-call(s32[2]{0:T(128)} %refs_0_.1, ...), custom_call_target="tpu_custom_call" | custom-call | tf_op jit(solution)/shard_map/layers/pallas_call | solution.py:1109
  264.4 8.1 %final.1 = (f32[2,128,768]{2,1,0:T(8,128)}, f32[2,128,768]{2,1,0:T(8,128)}, f32[192,768]{1,0:T(8,128)}, f32[192]{0:T(256)}, f32[192,768]{1,0:T(8,128)}, /*index=...) custom-call(bf16[2,128,768]{2,1,0:T(8,128)(2,1)} %get-tuple-element., ...), custom_call_target="tpu_custom_call" | custom-call | tf_op jit(solution)/shard_map/final/pallas_call | solution.py:1164

commit v3 on v2

--- a/solution.py
+++ b/solution.py
@@ -63,7 +63,9 @@
 class Gather:
     def __init__(self, me, shards, sems):
         self.me, self.shards = me, shards
-        self.zs, self.zr, self.ps, self.pr, self.fs, self.fr, self.ls = sems
+        self.zs, self.zr, self.ps, self.pr, self.fs, self.fr, self.ls, self.hs = sems
+        self.inner = jnp.logical_and(me.z >= 1, me.z <= 2)
+        self.across = {1: me.z != 3, 2: me.z >= 0, 3: me.z != 0}
 
     def only(self, w, cond):
         return (lambda f: pl.when(cond)(f)) if self.shards[w][2] == 2 else (lambda f: f())
@@ -84,16 +86,39 @@
             return dst.at[slot, rows_of(r, count), pl.ds(half * 384, 384)]
         return dst.at[slot, rows_of(2 * r + half, count // 2)]
 
-    def send(self, ws):
-        me = self.me
-        for w in ws:
-            src, dst, count = self.shards[w]
+    def begin(self, parts, ahead):
+        me = self.me
+        self.parts, self.ahead, self.turn = parts, ahead, 0
+        for w, (src, dst, count) in enumerate(self.shards):
 
             @self.only(w, me.z // 2 == me.c)
             def _():
-                for d in (2, 1, 3):
+                pltpu.make_async_copy(src, dst.at[self.slot(w, me.z)], self.ls.at[w]).start()
+
+        for i in range(ahead):
+            self.send(i)
+
+    def send(self, i):
+        me = self.me
+        if i >= len(self.parts):
+            return
+        for w, d in self.parts[i]:
+
+            @self.only(w, me.z // 2 == me.c)
+            def _():
+                @pl.when(self.across[d])
+                def _():
                     self.line_copy(w, d).start()
-                pltpu.make_async_copy(src, dst.at[self.slot(w, me.z)], self.ls.at[w]).start()
+
+    def advance(self, until):
+        while self.turn < until:
+            i = self.turn
+            if i < len(self.parts):
+                self.to_plane(self.parts[i])
+                self.send(i + self.ahead)
+            if 0 <= i - 1 < len(self.parts):
+                self.onward(self.parts[i - 1])
+            self.turn += 1
 
     def line_copy(self, w, d):
         me = self.me
@@ -105,6 +130,11 @@
             me.line(d),
         )
 
+    def end_copy(self, w):
+        me = self.me
+        ref = self.part(w, me.line_index(-2), me.r)
+        return remote(ref, ref, self.hs.at[w], self.zr.at[w, jnp.clip(2 * me.z - 2, 0, 2)], (me.r, jnp.clip(3 * (me.z - 1), 0, 3), me.s))
+
     def plane_copy(self, w, d, k):
         me = self.me
         ref = self.part(w, me.line_index(-d), me.r)
@@ -115,17 +145,22 @@
         ref = self.part(w, me.line_index(-d), me.plane_index(3 - k), k - 1)
         return remote(ref, ref, self.fs.at[w, d - 1, k - 1], self.fr.at[w, d - 1, k - 1], me.plane(k))
 
-    def each(self, ws, step):
-        for w in ws:
-            for d in (1, 2, 3):
-
-                @self.only(w, self.me.line_index(-d) // 2 == self.me.c)
-                def _():
-                    step(w, d)
+    def each(self, part, step):
+        for w, d in part:
+
+            @self.only(w, self.me.line_index(-d) // 2 == self.me.c)
+            def _():
+                step(w, d)
 
     def to_plane(self, ws):
         def step(w, d):
             self.line_copy(w, d).wait_recv()
+            if d == 2:
+
+                @pl.when(self.inner)
+                def _():
+                    self.end_copy(w).start()
+
             self.plane_copy(w, d, 1).start()
             self.plane_copy(w, d, 2).start()
 
@@ -144,7 +179,7 @@
             for k in (1, 2):
                 self.on_copy(w, d, k).wait_recv()
 
-        self.each(ws, step)
+        self.each([(w, d) for w in ws for d in (1, 2, 3)], step)
         for w in ws:
             src, dst, count = self.shards[w]
 
@@ -154,33 +189,46 @@
 
     def drain(self, ws):
         def step(w, d):
+            if d == 2:
+
+                @pl.when(self.inner)
+                def _():
+                    self.end_copy(w).wait_send()
+
             for k in (1, 2):
                 self.plane_copy(w, d, k).wait_send()
                 self.on_copy(w, d, k).wait_send()
 
-        self.each(ws, step)
+        self.each([(w, d) for w in ws for d in (1, 2, 3)], step)
         for w in ws:
 
             @self.only(w, self.me.z // 2 == self.me.c)
             def _():
                 for d in (1, 2, 3):
-                    self.line_copy(w, d).wait_send()
-
-
-HALVES, LINE, SPREAD = 0, 1, 2
+
+                    @pl.when(self.across[d])
+                    def _():
+                        self.line_copy(w, d).wait_send()
+
+
+PAIR, OWNER, EVERY = 0, 1, 2
+KINDS = (OWNER,) * 2 + (EVERY,) + (OWNER,) * 4 + (PAIR,) * 4
+
+
+def piece_shape(dims):
+    count, rows, cols = dims
+    return (count, rows // 4, cols // 2) if cols == 768 else (count, rows // 8, cols)
 
 
 class Reduce:
-    def __init__(self, me, grads, outs, bufs, sems):
-        self.me, self.grads, self.outs = me, grads, outs
+    def __init__(self, me, grads, outs, kinds, chunks, bufs, sems):
+        self.me, self.grads, self.outs, self.kinds, self.chunks = me, grads, outs, kinds, chunks
         self.RA, self.RB, self.RC, self.RD, self.RZ, self.SUM = bufs
         (self.as_, self.ar, self.bs, self.br, self.zs, self.zr, self.gs, self.gr, self.fs, self.fr, self.ls,
          self.cs, self.cr, self.ns, self.nr) = sems
         self.mx, self.my = lax.rem(me.r, 2), me.r // 2
         self.owner = me.z // 2 == me.c
-
-    def kind(self, w):
-        return {4: 1, 2: 0, 1: 2}[self.grads[w].shape[0]]
+        self.made = self.launched = self.turn = 0
 
     def quarter(self, w):
         return self.grads[w].shape[1] // 4
@@ -188,9 +236,9 @@
     def piece(self, w, t, half):
         g = self.grads[w]
         q, cols = self.quarter(w), g.shape[2]
-        if cols == 384:
-            return g.at[:, rows_of(2 * t + half, q // 2)]
-        return g.at[:, rows_of(t, q), pl.ds(half * (cols // 2), cols // 2)]
+        if cols == 768:
+            return g.at[:, rows_of(t, q), pl.ds(half * 384, 384)]
+        return g.at[:, rows_of(2 * t + half, q // 2)]
 
     def first_copy(self, w, half, other):
         if half == 0:
@@ -221,11 +269,8 @@
             self.piece(w, 2 * self.my + 1 - self.mx, 1), self.RD[w], self.bs.at[w, 1], self.br.at[w, 1], self.me.plane(1)
         )
 
-    def add_into(self, target, *more):
-        total = target[...].astype(F32)
-        for ref in more:
-            total = total + ref[...].astype(F32)
-        target[...] = total.astype(BF)
+    def add_into(self, target, ref):
+        target[...] = (target[...].astype(F32) + ref[...].astype(F32)).astype(BF)
 
     def second(self, ws):
         for w in ws:
@@ -246,7 +291,7 @@
             for half, land in ((0, self.RC), (1, self.RD)):
                 self.second_copy(w, half).wait()
                 self.add_into(self.piece(w, me.r, half), land[w])
-            if self.kind(w) == 0:
+            if self.kinds[w] == PAIR:
                 for u in range(2):
 
                     @pl.when(2 * me.c + u != me.z)
@@ -273,27 +318,23 @@
     def line_copy(self, w, d):
         me = self.me
         q = self.quarter(w)
-        if self.kind(w) == 1:
-            src = self.grads[w].at[me.line_index(d), rows_of(me.r, q)]
-        else:
-            src = self.grads[w].at[0, rows_of(me.r * 4 + me.line_index(d), q // 4)]
+        src = self.grads[w].at[me.line_index(d), rows_of(me.r, q)]
         return remote(src, self.RZ[w].at[d - 1], self.zs.at[w, d - 1], self.zr.at[w, d - 1], me.line(d))
 
     def near_copy(self, w, d):
-        mine = self.SUM[w].at[rows_of(self.me.z, self.quarter(w) // 4)]
-        return remote(mine, mine, self.ns.at[w - 8, d - 1], self.nr.at[w - 8, d - 1], self.me.line(d))
-
-    def out(self, w):
-        return self.outs[w].at[0] if self.kind(w) == 2 else self.outs[w]
+        mine = self.SUM[w].at[self.me.z]
+        return remote(mine, mine, self.ns.at[w, d - 1], self.nr.at[w, d - 1], self.me.line(d))
 
     def out_part(self, w, t, half=None):
-        out, q = self.out(w), self.quarter(w)
-        cols = out.shape[1]
+        out, q = self.outs[w], self.quarter(w)
+        if self.kinds[w] == EVERY:
+            rows = rows_of(t, q) if half is None else rows_of(2 * t + half, q // 2)
+            return out.at[0, :, rows]
         if half is None:
             return out.at[rows_of(t, q)]
-        if cols == 384:
-            return out.at[rows_of(2 * t + half, q // 2)]
-        return out.at[rows_of(t, q), pl.ds(half * (cols // 2), cols // 2)]
+        if out.shape[1] == 768:
+            return out.at[rows_of(t, q), pl.ds(half * 384, 384)]
+        return out.at[rows_of(2 * t + half, q // 2)]
 
     def plane_copy(self, w, k):
         me = self.me
@@ -307,12 +348,12 @@
         return pltpu.make_async_copy(self.SUM[w], self.out_part(w, self.me.r), self.ls.at[w])
 
     def core_copy(self, w):
-        if self.kind(w) == 2:
+        if self.kinds[w] == EVERY:
             return remote(self.outs[w].at[0], self.outs[w].at[1], self.cs.at[w], self.cr.at[w], self.me.core())
         return remote(self.outs[w], self.outs[w], self.cs.at[w], self.cr.at[w], self.me.core())
 
     def only(self, w):
-        return (lambda f: pl.when(self.owner)(f)) if self.kind(w) == 0 else (lambda f: f())
+        return (lambda f: pl.when(self.owner)(f)) if self.kinds[w] == PAIR else (lambda f: f())
 
     def spread_start(self, w):
         self.own_copy(w).start()
@@ -323,7 +364,8 @@
         me = self.me
         for w in ws:
             q = self.quarter(w)
-            if self.kind(w) == 0:
+            kind = self.kinds[w]
+            if kind == PAIR:
                 for u in range(2):
 
                     @pl.when(2 * me.c + u != me.z)
@@ -341,16 +383,15 @@
                 continue
             for d in (1, 2, 3):
                 self.line_copy(w, d).wait()
-            if self.kind(w) == 1:
-                own = self.grads[w].at[me.z, rows_of(me.r, q)]
-                self.SUM[w][...] = add_up([own] + [self.RZ[w].at[d] for d in range(3)]).astype(BF)
-                self.spread_start(w)
-            else:
-                own = self.grads[w].at[0, rows_of(me.r * 4 + me.z, q // 4)]
-                total = add_up([own] + [self.RZ[w].at[d] for d in range(3)]).astype(BF)
-                self.SUM[w][rows_of(me.z, q // 4)] = total
+            own = self.grads[w].at[me.z, rows_of(me.r, q)]
+            total = add_up([own] + [self.RZ[w].at[d] for d in range(3)]).astype(BF)
+            if kind == EVERY:
+                self.SUM[w][me.z] = total
                 for d in (1, 2, 3):
                     self.near_copy(w, d).start()
+            else:
+                self.SUM[w][...] = total
+                self.spread_start(w)
 
     def spread_near(self, ws):
         for w in ws:
@@ -375,12 +416,12 @@
                 self.own_copy(w).wait()
                 for k in (1, 2):
                     self.on_copy(w, k).wait()
-                if self.kind(w) != 1:
+                if self.kinds[w] != OWNER:
                     self.core_copy(w).start()
 
-    def end(self, ws):
-        for w in ws:
-            if self.kind(w) == 0:
+    def end(self):
+        for w, kind in enumerate(self.kinds):
+            if kind == PAIR:
 
                 @pl.when(self.owner)
                 def _():
@@ -390,8 +431,37 @@
                 def _():
                     self.core_copy(w).wait_recv()
 
-            elif self.kind(w) == 2:
+            elif kind == EVERY:
                 self.core_copy(w).wait()
+
+    def launch(self, upto):
+        while self.launched < min(upto, self.made, len(self.chunks)):
+            self.start(self.chunks[self.launched])
+            self.launched += 1
+
+    def ready(self, made, ahead):
+        self.made = made
+        self.launch(self.turn + ahead)
+
+    def step(self, ahead):
+        i = self.turn
+
+        def at(back, every=None):
+            chunk = self.chunks[i - back] if 0 <= i - back < len(self.chunks) else ()
+            return [w for w in chunk if every is None or every == (self.kinds[w] == EVERY)]
+
+        self.second(at(0))
+        self.turn += 1
+        self.launch(self.turn + ahead)
+        self.along(at(1))
+        self.spread(at(2))
+        self.spread_near(at(3, True))
+        self.onward(at(3, False) + at(4, True))
+        self.finish(at(4, False) + at(5, True))
+
+    def rest(self, ahead):
+        while self.turn < len(self.chunks) + 4:
+            self.step(ahead)
 
 
 def add_up(refs):
@@ -578,6 +648,7 @@
     units = L.q.shape[0]
     prow = L.prow
     n_rows = L.x.shape[0]
+    hook("start")
     for i in range(6):
         sums[prow + i : prow + i + 1, :] = jnp.zeros((1, 768), F32)
 
@@ -600,7 +671,9 @@
         L.gp[j] = dpre
         n = dpre.shape[1]
         sums[pl.ds(L.brow + j, 1), :n] = col_sum(dpre.astype(F32))
-
+        L.wf[j] = tn(L.g[j], L.dr[...]).astype(BF)
+
+    hook("out_grads")
     leave = nn if L.flip_in else nt
 
     def ffn_part(rows):
@@ -612,7 +685,6 @@
     def ffn_weights():
         @pl.loop(0, 4)
         def _(j):
-            L.wf[j] = tn(L.g[j], L.dr[...]).astype(BF)
             if L.flip_in:
                 L.wi[j] = tn(L.gp[j], L.a[...]).astype(BF)
             else:
@@ -672,13 +744,20 @@
         return total
 
     def attn_weights():
+        if L.pack is not None:
+            L.pack()
+            sums[L.qrow : L.qrow + 1, :256] = col_sum(L.dq[0].astype(F32))
+            sums[L.qrow + 1 : L.qrow + 2, :256] = col_sum(L.dv[0].astype(F32))
+            hook("attn_grads")
+            return
+
         @pl.loop(0, units)
         def _(u):
             n = L.width
             L.wo[u] = tn(L.o[u, :, :n], L.dr[...]).astype(BF)
             x = L.x[...]
             for grad, out in ((L.dq, L.wq), (L.dk, L.wk), (L.dv, L.wv)):
-                out[u] = (tn(grad[u, :, :n], x) if L.flip_attn else tn(x, grad[u, :, :n])).astype(BF)
+                out[u] = tn(grad[u, :, :n], x).astype(BF)
             sums[pl.ds(L.qrow + u, 1), :256] = col_sum(L.dq[u].astype(F32))
             sums[pl.ds(L.qrow + units + u, 1), :256] = col_sum(L.dv[u].astype(F32))
 
@@ -802,23 +881,23 @@
     vectors = refs[15:27]
     sqb, svb, tqb, tvb, tib, sib = refs[27:33]
     (YO, DO, SUMS) = refs[33:36]
-    outs = refs[36:48]
-    rest = list(refs[48:])
+    outs = refs[36:45]
+    rest = list(refs[45:])
 
     def take(count):
         head, rest[:] = rest[:count], rest[count:]
         return head
 
     WQ, WK, WV, WO, WI, WF, SI, SF, wsq, wsk, wsv, wso = weights = take(12)
-    X, CT, LN, PACK, BP, PRM, SM, sml = take(8)
+    X, CT, LN, PACK, BP, PRM, SM, sml, both, SG, BX, RBX = take(12)
     bias_row, send, recv, ssem, rsem = take(5)
     q, k, v, o, p, xh1, rs1, a, g, gp, xh2, rs2, df, dr, do, dq, dk, dv, ds = take(19)
     x2, q2, k2, v2, o2, p2, xh12, rs12, a2, g2, gp2, xh22, rs22, dx2, Y, DX = take(16)
-    bufs = [take(12) for _ in range(6)]
-    gather_sems = take(7)
+    bufs = [take(len(KINDS)) for _ in range(6)]
+    gather_sems = take(8)
     reduce_sems = take(15)
     seq_sems, home_sems = take(4), take(2)
-    pks, pkr, lcs, lcr, sls, sms, smr = take(7)
+    pks, pkr, lcs, lcr, sls, sms, smr, hcs, hcr = take(9)
 
     LN[0] = jnp.full(LN.shape[1:], lens[z % 2].astype(F32))
     PACK[...] = jnp.zeros(PACK.shape, F32)
@@ -836,14 +915,18 @@
         ((tq, WQ, 2), (tk, WK, 2), (tv, WV, 2), (to, WO, 2), (ti, WI, 4), (tf, WF, 4), (si, SI, 4), (sf, SF, 4)),
         gather_sems,
     )
-    G0, G1, G2, G3 = (0, 1, 2), (3, 4), (5,), (6, 7)
-
-    sequences.send(0)
+
     pack_copies = [remote(PACK, BP.at[z], pks.at[d - 1], pkr.at[d - 1], me.line(d)) for d in (1, 2, 3)]
     for copy in pack_copies:
         copy.start()
-    gather.send(G0)
-    gather.send(G1)
+    far_first = (2, 1, 3)
+    gather.begin(
+        [[(w, d) for d in far_first] for w in (0, 1, 2, 3)]
+        + [[(4, d)] for d in far_first]
+        + [[(5, d)] for d in far_first]
+        + [[(w, d) for d in far_first] for w in (6, 7)],
+        3,
+    )
     lens_copy = remote(LN.at[0], LN.at[1], lcs.at[0], lcr.at[0], me.core())
 
     @pl.when(owner)
@@ -889,7 +972,7 @@
         bias_q=lambda u: BP[2 * c + u, 0:1, 0:192],
         bias_v=lambda u: BP[2 * c + u, 3:4, 0:192],
         bias_i=lambda j: BP[j, 1:2, :],
-        third=lambda c: 0,
+        third=lambda c: 0, pack=None,
     )
     student = Layer(
         x=x2, wq=wsq, wk=wsk, wv=wsv, wo=wso, wi=SI, wf=SF, q=q2, k=k2, v=v2, o=o2, p=p2, xh1=xh12, rs1=rs12, a=a2,
@@ -898,43 +981,64 @@
         bias_q=lambda u: jnp.concatenate([PRM[12:13, s_bias], PRM[12:13, 128:256]], axis=1),
         bias_v=lambda u: jnp.concatenate([PRM[12:13, v_bias], PRM[12:13, 512:640]], axis=1),
         bias_i=lambda j: BP[j, 2:3, 0 : SI.shape[1]],
-        third=lambda c: c,
+        third=lambda c: c, pack=lambda: pack_student(),
     )
     swap = Swap(me, send, recv, ssem, rsem, 4)
+    far_half, near_half = rows_of(1 - c, 384), rows_of(c, 384)
+    half_copy = remote(BX.at[:, far_half], RBX, hcs.at[0], hcr.at[0], me.core())
+
+    def pack_student():
+        x = x2[...]
+        for i, grad in enumerate((dq, dk, dv)):
+            value = tn(x, grad[0]).astype(BF)
+            SG[i, 0:768] = value[:, 0:128]
+            BX[i] = value[:, 128:256]
+        value = tn(o2[0], dr[...]).astype(BF)
+        for b in range(6):
+            cols = slice(128 * b, 128 * b + 128)
+            SG[3, 128 * b : 128 * b + 128] = value[0:128, cols]
+            for h in range(2):
+                BX[3, 384 * h + 64 * b : 384 * h + 64 * b + 64] = value[128 + 64 * h : 192 + 64 * h, cols]
+        half_copy.start()
+
+    def join_halves():
+        half_copy.wait()
+        SG[:, 768:1152] = (BX[:, near_half].astype(F32) + RBX[...].astype(F32)).astype(BF)
 
     def teacher_hook(name):
         if name == "qkv":
+            gather.advance(3)
+            sequences.send(0)
+            gather.advance(6)
             sequences.take(0)
-            gather.to_plane(G0)
-            gather.onward(G0)
-            gather.to_plane(G1[:1])
+            gather.advance(7)
             for copy in pack_copies:
                 copy.wait()
             for copy in local:
                 copy.wait()
-            gather.ready(G0)
+            gather.ready((0, 1, 2))
         if name == "heads":
-            gather.send(G2)
-            gather.onward(G1[:1])
-            gather.to_plane(G1[1:])
+            gather.advance(7)
         if name == "middle":
-            gather.onward(G1[1:])
-            gather.send(G3)
-            gather.to_plane(G2)
+            gather.advance(9)
         if name == "attn":
-            gather.onward(G2)
-            gather.to_plane(G3)
+            gather.advance(10)
+            gather.ready((3,))
             sequences.send(1)
-            gather.ready(G1[:1])
         if name == "ffn_in":
-            gather.ready(G1[1:])
+            gather.advance(11)
+            gather.ready((4,))
         if name == "ffn_out":
-            gather.onward(G3)
-            gather.ready(G2)
+            gather.advance(12)
+            gather.ready((5,))
 
     def student_hook(name):
+        if name == "qkv":
+            gather.advance(13)
         if name == "ffn_in":
-            gather.ready(G3)
+            gather.ready((6,))
+        if name == "ffn_out":
+            gather.ready((7,))
             sequences.take(1)
 
     def to_student(rows, value):
@@ -956,65 +1060,64 @@
     sequences.drain(0)
     sequences.drain(1)
 
-    total = Reduce(me, weights, outs, bufs, reduce_sems)
-    R0, R1, R2, R3 = (6, 7), (8, 9, 10, 11), (4, 5), (0, 1, 2, 3)
+    low, high = pl.ds(0, WF.shape[1] // 2), pl.ds(WF.shape[1] // 2, WF.shape[1] // 2)
+    top, bottom = pl.ds(0, 384), pl.ds(384, 384)
+    grads = [SF, SI, SG, WF.at[:, low], WF.at[:, high], WI.at[:, top], WI.at[:, bottom], WQ, WK, WV, WO]
+    lands = [outs[7], outs[6], outs[8], outs[5].at[low], outs[5].at[high], outs[4].at[top], outs[4].at[bottom],
+             outs[0], outs[1], outs[2], outs[3]]
+    total = Reduce(
+        me, grads, lands, KINDS, ((0,), (1,), (2,), (3,), (4,), (5,), (6,), (10,), (7, 8), (9,)), bufs, reduce_sems
+    )
+    AHEAD = 2
 
     def student_back(name):
+        if name == "out_grads":
+            total.ready(1, AHEAD)
         if name == "ffn_grads":
-            total.start(R0)
+            total.ready(2, AHEAD)
+
+    def teacher_back(name):
+        if name == "start":
+            join_halves()
+            total.ready(3, 3)
+            total.step(AHEAD)
+        if name == "out_grads":
+            total.ready(5, 3)
+        if name == "ffn_grads":
+            total.ready(7, 3)
+        if name == "attn":
+            total.step(AHEAD)
+        if name == "heads_done":
+            total.step(AHEAD)
+            total.step(AHEAD)
         if name == "attn_grads":
-            total.start(R1)
-
-    def teacher_back(name):
-        if name == "ffn_grads":
-            total.start(R2)
-            total.second(R0)
-            total.second(R1)
-        if name == "heads_done":
-            total.along(R0)
-            total.along(R1)
-        if name == "attn_grads":
-            total.start(R3)
+            total.ready(10, AHEAD)
 
     backward(student, me, swap, PRM, SM, lambda rows: CT[rows].astype(F32), student_back, between)
     backward(teacher, me, swap, PRM, SM, lambda rows: dx2[rows], teacher_back, to_grad)
     home.send(1)
 
-    sml[0] = SM[...]
+    sml[0] = SM[...].astype(BF)
     for d in (1, 2, 3):
         remote(sml.at[0], sml.at[d], sms.at[d - 1], smr.at[d - 1], me.line(d)).start()
-    total.spread(R0)
-    total.spread(R1)
-    total.second(R2)
-    total.second(R3)
-    total.spread_near(R1)
+    total.step(AHEAD)
     for d in (1, 2, 3):
         remote(sml.at[0], sml.at[d], sms.at[d - 1], smr.at[d - 1], me.line(d)).wait()
-    sml[4] = add_up([sml.at[i] for i in range(4)])
+    sml[4] = add_up([sml.at[i] for i in range(4)]).astype(BF)
     for k in (1, 2, 3):
         remote(sml.at[4], sml.at[4 + k], sms.at[2 + k], smr.at[2 + k], me.plane(k)).start()
-    total.onward(R0)
-    total.along(R2)
-    total.along(R3)
-    total.onward(R1)
+    total.step(AHEAD)
     for k in (1, 2, 3):
         remote(sml.at[4], sml.at[4 + k], sms.at[2 + k], smr.at[2 + k], me.plane(k)).wait()
-    sml[8] = add_up([sml.at[4 + i] for i in range(4)])
-    other_sums = remote(sml.at[8], sml.at[9], sms.at[6], smr.at[6], me.core())
+    both[0] = add_up([sml.at[4 + i] for i in range(4)])
+    other_sums = remote(both.at[0], both.at[1], sms.at[6], smr.at[6], me.core())
     other_sums.start()
-    total.spread(R2)
-    total.finish(R0)
-    total.finish(R1)
-    total.spread(R3)
-    total.onward(R2)
-    total.onward(R3)
+    total.step(AHEAD)
     other_sums.wait()
-    both_sums = pltpu.make_async_copy(sml.at[pl.ds(8, 2)], SUMS, sls.at[9])
+    both_sums = pltpu.make_async_copy(both, SUMS, sls.at[9])
     both_sums.start()
-    total.finish(R2)
-    total.finish(R3)
-    total.end(R1)
-    total.end(R3)
+    total.rest(AHEAD)
+    total.end()
     home.drain(0)
     home.drain(1)
     both_sums.wait()
@@ -1024,23 +1127,24 @@
     z = lax.axis_index("head")
     c = lax.rem(lax.axis_index("seq"), 2)
     YO, DO, SUMS = refs[:3]
-    grads = refs[3:15]
-    outs = refs[15:]
+    grads = refs[3:12]
+    outs = refs[12:]
     outs[0][...] = YO[...].astype(F32)
     outs[1][...] = DO[...].astype(F32)
     for at, w in ((2, 0), (4, 1), (5, 2), (7, 3), (11, 4), (13, 5), (26, 6), (28, 7)):
         outs[at][...] = grads[w][...].astype(F32)
     near = pl.ds(pl.multiple_of(c * 256, 128), 128)
     far = pl.ds(pl.multiple_of((1 - c) * 256, 128), 128)
-    for at, w in ((17, 8), (19, 9), (20, 10)):
-        g = grads[w]
-        outs[at][:, near] = g[0, :, 0:128].astype(F32)
-        outs[at][:, far] = g[1, :, 0:128].astype(F32)
-        outs[at][:, 128:256] = g[0, :, 128:256].astype(F32) + g[1, :, 128:256].astype(F32)
-    g = grads[11]
-    outs[22][near, :] = g[0, 0:128, :].astype(F32)
-    outs[22][far, :] = g[1, 0:128, :].astype(F32)
-    outs[22][128:256, :] = g[0, 128:256, :].astype(F32) + g[1, 128:256, :].astype(F32)
+    packed = grads[8]
+    for i, at in enumerate((17, 19, 20)):
+        for side, cols, half in ((0, near, c), (1, far, 1 - c)):
+            outs[at][:, cols] = packed[side, i, 0:768].astype(F32)
+            outs[at][rows_of(half, 384), 128:256] = packed[side, i, 768:1152].astype(F32)
+    for side, first, half in ((0, near, c), (1, far, 1 - c)):
+        for b in range(6):
+            cols = pl.ds(128 * b, 128)
+            outs[22][first, cols] = packed[side, 3, 128 * b : 128 * b + 128].astype(F32)
+            outs[22][pl.ds(128 + 64 * half, 64), cols] = packed[side, 3, 768 + 64 * b : 832 + 64 * b].astype(F32)
 
     def put(at, value):
         outs[at][...] = value.reshape(value.shape[1])
@@ -1098,23 +1202,22 @@
     ]
     names = len(weights)
 
-    def piece(w):
-        count, rows, cols = weights[w]
-        return (count, rows // 8, cols) if cols == 384 else (count, rows // 4, cols // 2)
-
-    def share(w):
-        count, rows, cols = weights[w]
-        return (rows // 16 if count == 1 else rows // 4, cols)
+    parts = [weights[7], weights[6], (4, 1152, 128), (4, n_in // 2, 768), (4, n_in // 2, 768), (4, 384, n_in), (4, 384, n_in),
+             weights[0], weights[1], weights[2], weights[3]]
+    pieces = [piece_shape(dims) for dims in parts]
+    many = len(parts)
 
     results = pl.pallas_call(
         main_kernel,
         out_shape=[shape(2, 128, 768), shape(2, 128, 768), shape(2, 32, 768, kind=F32)]
-        + [shape(2, *d[1:]) if d[0] == 1 else shape(*d[1:]) for d in weights],
+        + [shape(*d[1:]) for d in weights[:8]]
+        + [shape(2, 4, 1152, 128)],
         in_specs=[pl.BlockSpec(memory_space=pltpu.SMEM)] + [ANYWHERE] * 14 + [IN_VMEM] * 18,
-        out_specs=[ANYWHERE] * (3 + names),
+        out_specs=[ANYWHERE] * 12,
         scratch_shapes=[act(*d) for d in weights]
         + [
-            act(n, 768), act(n, 768), wide(2, 8, 128), wide(8, n_in), wide(4, 8, n_in), wide(16, 768), wide(32, 768), wide(10, 32, 768),
+            act(n, 768), act(n, 768), wide(2, 8, 128), wide(8, n_in), wide(4, 8, n_in), wide(16, 768), wide(32, 768), act(8, 32, 768), wide(2, 32, 768),
+            act(4, 1152, 128), act(4, 768, 128), act(4, 384, 128),
             wide(8, n), act(2, n, 768), act(2, n, 768), dma((2, 4)), dma((2, 4)),
             act(2, n, 256), act(2, n, 256), act(2, n, 256), act(2, n, 256), act(6, n, n),
             wide(n, 768), wide(n, 1), act(n, 768), act(4, n, n_in), act(4, n, n_in), wide(n, 768), wide(n, 1),
@@ -1123,19 +1226,19 @@
             wide(n, 768), wide(n, 1), act(n, 768), act(4, n, n_s), act(4, n, n_s), wide(n, 768), wide(n, 1),
             wide(n, 768), act(n, 768), act(n, 768),
         ]
-        + [act(2, *piece(w)) for w in range(names)]
-        + [act(2, *piece(w)) for w in range(names)]
-        + [act(*piece(w)) for w in range(names)]
-        + [act(*piece(w)) for w in range(names)]
-        + [act(3, *share(w)) for w in range(names)]
-        + [act(weights[w][1] // 4, weights[w][2]) for w in range(names)]
+        + [act(2, *p) for p in pieces]
+        + [act(2, *p) for p in pieces]
+        + [act(*p) for p in pieces]
+        + [act(*p) for p in pieces]
+        + [act(3, dims[1] // 4, dims[2]) for dims in parts]
+        + [act(4, 288, 128) if kind == EVERY else act(d[1] // 4, d[2]) for d, kind in zip(parts, KINDS)]
         + [
-            dma((8, 3)), dma((8, 3)), dma((8, 3, 2)), dma((8, 3, 2)), dma((8, 3, 2)), dma((8, 3, 2)), dma((8,)),
-            dma((names, 4)), dma((names, 4)), dma((names, 2)), dma((names, 2)), dma((names, 3)), dma((names, 3)),
-            dma((names, 2)), dma((names, 2)), dma((names, 2)), dma((names, 2)), dma((names,)), dma((names,)), dma((names,)),
-            dma((4, 3)), dma((4, 3)),
+            dma((8, 3)), dma((8, 3)), dma((8, 3, 2)), dma((8, 3, 2)), dma((8, 3, 2)), dma((8, 3, 2)), dma((8,)), dma((8,)),
+            dma((many, 4)), dma((many, 4)), dma((many, 2)), dma((many, 2)), dma((many, 3)), dma((many, 3)),
+            dma((many, 2)), dma((many, 2)), dma((many, 2)), dma((many, 2)), dma((many,)), dma((many,)), dma((many,)),
+            dma((many, 3)), dma((many, 3)),
             dma((2, 2)), dma((2, 4)), dma((2, 4)), dma((2, 4)), dma((2, 3)), dma((2, 2)),
-            dma((3,)), dma((3,)), dma((1,)), dma((1,)), dma((10,)), dma((7,)), dma((7,)),
+            dma((3,)), dma((3,)), dma((1,)), dma((1,)), dma((10,)), dma((7,)), dma((7,)), dma((1,)), dma((1,)),
         ],
         compiler_params=pltpu.CompilerParams(collective_id=0, has_side_effects=True, vmem_limit_bytes=VMEM_LIMIT),
         name="layers",
@@ -1164,7 +1267,7 @@
         pl.pallas_call(
             final_kernel,
             out_shape=final_shapes,
-            in_specs=[IN_VMEM] * (3 + names),
+            in_specs=[IN_VMEM] * 12,
             out_specs=[IN_VMEM] * len(final_shapes),
             compiler_params=pltpu.CompilerParams(vmem_limit_bytes=VMEM_LIMIT),
             name="final",

time: 273 us -> 245 us (0.90)
  Pallas kernels: 272 us -> 244 us
    pallas_call x1, Pallas kernels: 264 us -> 236 us  [body(): pl.pallas_call(main_kernel, out_shape=[shape(2, 128, 768), shape(2, 128,...]
where the time goes in v3:
time: 245 us
  Pallas kernels  244 us (100%)
    pallas_call x1, Pallas kernels, body(): pl.pallas_call(main_kernel, out_shape=[shape(2, 128, 768), shape(2, 128,...  236 us
    pallas_call x1, Pallas kernels, body(): pl.pallas_call(final_kernel, out_shape=final_shapes, in_specs=[IN_VMEM] *...  8.01 us

profile of v3, /device:TPU:0, one launch (start us, length us, event | category | flops | bytes accessed | tf_op | source)
XLA Modules:
  0.0 245.0 jit_solution(1387387712799786392)
XLA Ops:
  0.7 236.1 %layers.1 = (bf16[2,128,768]{2,1,0:T(8,128)(2,1)}, bf16[2,128,768]{2,1,0:T(8,128)(2,1)}, f32[2,32,768]{2,1,0:T(8,128)}, bf16[192,768]{1,0:T(8,128)(2,1)}, bf16[1...) custom-call(s32[2]{0:T(128)} %refs_0_.1, ...), custom_call_target="tpu_custom_call" | custom-call | tf_op jit(solution)/shard_map/layers/pallas_call | solution.py:1210
  236.8 8.0 %final.1 = (f32[2,128,768]{2,1,0:T(8,128)}, f32[2,128,768]{2,1,0:T(8,128)}, f32[192,768]{1,0:T(8,128)}, f32[192]{0:T(256)}, f32[192,768]{1,0:T(8,128)}, /*index=...) custom-call(bf16[2,128,768]{2,1,0:T(8,128)(2,1)} %get-tuple-element., ...), custom_call_target="tpu_custom_call" | custom-call | tf_op jit(solution)/shard_map/final/pallas_call | solution.py:1267

commit v4 on v3

--- a/solution.py
+++ b/solution.py
@@ -445,6 +445,8 @@
 
     def step(self, ahead):
         i = self.turn
+        if self.made <= i < len(self.chunks):
+            return
 
         def at(back, every=None):
             chunk = self.chunks[i - back] if 0 <= i - back < len(self.chunks) else ()
@@ -715,22 +717,27 @@
         for ref in (L.dq, L.dk, L.dv):
             ref[u] = jnp.zeros(ref.shape[1:], BF)
 
-    @pl.loop(0, 3 * units)
-    def _(i):
-        u, cols, mask = head_mask(L, i, c)
-        k = L.k[u, :, cols] * mask
-        v = L.v[u, :, cols]
-        for ch in range(4):
-            rows = pl.ds(ch * 128, 128)
-            d_probs = nt(L.do[u, rows, cols] * mask, v)
-            probs = L.p[i, rows].astype(F32)
-            both = probs * d_probs
-            d_scores = (both - probs * jnp.sum(both, axis=-1, keepdims=True)).astype(BF)
-            L.ds[rows] = d_scores
-            L.dq[u, rows, cols] = L.dq[u, rows, cols] + (nn(d_scores, k) * 0.125).astype(BF)
-        L.dv[u, :, cols] = L.dv[u, :, cols] + tn(L.p[i], L.do[u, :, cols] * mask).astype(BF)
-        L.dk[u, :, cols] = L.dk[u, :, cols] + tn(L.ds[...], L.q[u, :, cols] * mask).astype(BF)
-
+    def heads(lo, hi):
+        @pl.loop(lo, hi)
+        def _(i):
+            u, cols, mask = head_mask(L, i, c)
+            k = L.k[u, :, cols] * mask
+            v = L.v[u, :, cols]
+            for ch in range(4):
+                rows = pl.ds(ch * 128, 128)
+                d_probs = nt(L.do[u, rows, cols] * mask, v)
+                probs = L.p[i, rows].astype(F32)
+                both = probs * d_probs
+                d_scores = (both - probs * jnp.sum(both, axis=-1, keepdims=True)).astype(BF)
+                L.ds[rows] = d_scores
+                L.dq[u, rows, cols] = L.dq[u, rows, cols] + (nn(d_scores, k) * 0.125).astype(BF)
+            L.dv[u, :, cols] = L.dv[u, :, cols] + tn(L.p[i], L.do[u, :, cols] * mask).astype(BF)
+            L.dk[u, :, cols] = L.dk[u, :, cols] + tn(L.ds[...], L.q[u, :, cols] * mask).astype(BF)
+
+    heads(0, 3)
+    if units == 2:
+        hook("middle")
+        heads(3, 6)
     hook("heads_done")
     back = nn if L.flip_attn else nt
 
@@ -1066,32 +1073,33 @@
     lands = [outs[7], outs[6], outs[8], outs[5].at[low], outs[5].at[high], outs[4].at[top], outs[4].at[bottom],
              outs[0], outs[1], outs[2], outs[3]]
     total = Reduce(
-        me, grads, lands, KINDS, ((0,), (1,), (2,), (3,), (4,), (5,), (6,), (10,), (7, 8), (9,)), bufs, reduce_sems
+        me, grads, lands, KINDS, ((0, 1), (2,), (3, 4), (5, 6), (7, 8, 9, 10)), bufs, reduce_sems
     )
     AHEAD = 2
 
     def student_back(name):
         if name == "out_grads":
+            total.ready(0, AHEAD)
+        if name == "ffn_grads":
             total.ready(1, AHEAD)
-        if name == "ffn_grads":
-            total.ready(2, AHEAD)
 
     def teacher_back(name):
         if name == "start":
             join_halves()
-            total.ready(3, 3)
+            total.ready(2, AHEAD)
             total.step(AHEAD)
         if name == "out_grads":
-            total.ready(5, 3)
+            total.ready(3, AHEAD)
         if name == "ffn_grads":
-            total.ready(7, 3)
+            total.ready(4, AHEAD)
         if name == "attn":
+            total.step(AHEAD)
+        if name == "middle":
             total.step(AHEAD)
         if name == "heads_done":
             total.step(AHEAD)
-            total.step(AHEAD)
         if name == "attn_grads":
-            total.ready(10, AHEAD)
+            total.ready(5, AHEAD)
 
     backward(student, me, swap, PRM, SM, lambda rows: CT[rows].astype(F32), student_back, between)
     backward(teacher, me, swap, PRM, SM, lambda rows: dx2[rows], teacher_back, to_grad)

time: 245 us -> 239 us (0.976)
  Pallas kernels: 244 us -> 238 us
    pallas_call x1, Pallas kernels: 236 us -> 230 us  [body(): pl.pallas_call(main_kernel, out_shape=[shape(2, 128, 768), shape(2, 128,...]
where the time goes in v4:
time: 239 us
  Pallas kernels  238 us (100%)
    pallas_call x1, Pallas kernels, body(): pl.pallas_call(main_kernel, out_shape=[shape(2, 128, 768), shape(2, 128,...  230 us
    pallas_call x1, Pallas kernels, body(): pl.pallas_call(final_kernel, out_shape=final_shapes, in_specs=[IN_VMEM] *...  8.01 us

profile of v4, /device:TPU:0, one launch (start us, length us, event | category | flops | bytes accessed | tf_op | source)
XLA Modules:
  0.0 238.8 jit_solution(7646755595301475091)
XLA Ops:
  0.7 229.9 %layers.1 = (bf16[2,128,768]{2,1,0:T(8,128)(2,1)}, bf16[2,128,768]{2,1,0:T(8,128)(2,1)}, f32[2,32,768]{2,1,0:T(8,128)}, bf16[192,768]{1,0:T(8,128)(2,1)}, bf16[1...) custom-call(s32[2]{0:T(128)} %refs_0_.1, ...), custom_call_target="tpu_custom_call" | custom-call | tf_op jit(solution)/shard_map/layers/pallas_call | solution.py:1218
  230.6 8.0 %final.1 = (f32[2,128,768]{2,1,0:T(8,128)}, f32[2,128,768]{2,1,0:T(8,128)}, f32[192,768]{1,0:T(8,128)}, f32[192]{0:T(256)}, f32[192,768]{1,0:T(8,128)}, /*index=...) custom-call(bf16[2,128,768]{2,1,0:T(8,128)(2,1)} %get-tuple-element., ...), custom_call_target="tpu_custom_call" | custom-call | tf_op jit(solution)/shard_map/final/pallas_call | solution.py:1275

commit v5 on v4

--- a/solution.py
+++ b/solution.py
@@ -1031,12 +1031,12 @@
         if name == "attn":
             gather.advance(10)
             gather.ready((3,))
-            sequences.send(1)
         if name == "ffn_in":
             gather.advance(11)
             gather.ready((4,))
         if name == "ffn_out":
             gather.advance(12)
+            sequences.send(1)
             gather.ready((5,))
 
     def student_hook(name):
@@ -1046,7 +1046,6 @@
             gather.ready((6,))
         if name == "ffn_out":
             gather.ready((7,))
-            sequences.take(1)
 
     def to_student(rows, value):
         x2[rows] = value.astype(BF)
@@ -1062,6 +1061,7 @@
 
     forward(teacher, me, swap, bias_row, PRM, teacher_hook, to_student)
     forward(student, me, swap, bias_row, PRM, student_hook, to_output)
+    sequences.take(1)
     home.send(0)
     gather.drain(range(8))
     sequences.drain(0)

time: 239 us -> 238 us (level)
  no operation moved by 1% of the time
where the time goes in v5:
time: 238 us; the launch traced here: 237 us
  Pallas kernels  236 us (99%)
    pallas_call x1, Pallas kernels, body(): pl.pallas_call(main_kernel, out_shape=[shape(2, 128, 768), shape(2, 128,...  228 us
    pallas_call x1, Pallas kernels, body(): pl.pallas_call(final_kernel, out_shape=final_shapes, in_specs=[IN_VMEM] *...  8.01 us

profile of v5, /device:TPU:0, one launch (start us, length us, event | category | flops | bytes accessed | tf_op | source)
XLA Modules:
  0.0 237.3 jit_solution(362955987224593172)
XLA Ops:
  0.7 228.4 %layers.1 = (bf16[2,128,768]{2,1,0:T(8,128)(2,1)}, bf16[2,128,768]{2,1,0:T(8,128)(2,1)}, f32[2,32,768]{2,1,0:T(8,128)}, bf16[192,768]{1,0:T(8,128)(2,1)}, bf16[1...) custom-call(s32[2]{0:T(128)} %refs_0_.1, ...), custom_call_target="tpu_custom_call" | custom-call | tf_op jit(solution)/shard_map/layers/pallas_call | solution.py:1218
  229.1 8.0 %final.1 = (f32[2,128,768]{2,1,0:T(8,128)}, f32[2,128,768]{2,1,0:T(8,128)}, f32[192,768]{1,0:T(8,128)}, f32[192]{0:T(256)}, f32[192,768]{1,0:T(8,128)}, /*index=...) custom-call(bf16[2,128,768]{2,1,0:T(8,128)(2,1)} %get-tuple-element., ...), custom_call_target="tpu_custom_call" | custom-call | tf_op jit(solution)/shard_map/final/pallas_call | solution.py:1275
